TPU v7x, 32 devices: a whole 2x2x4 slice. The times are simulated.
32 devices in a mesh: temporal: 16 (over z, y, core), ulysses: 2 (over x).
Axes of the slice: x: 2, y: 2, z: 4, core: 2. Of those that a mesh axis runs over, the one named last changes fastest.
Arguments:
- queries: bfloat16 [16384, 1536], P(('temporal', 'ulysses')), may hold values from -12 to 12
- keys: bfloat16 [16384, 1536], P(('temporal', 'ulysses')), may hold values from -12 to 12
- values: bfloat16 [16384, 1536], P(('temporal', 'ulysses')), may hold values from -6 to 6
- tile_list: int32 [128, 5], P('temporal'), may hold values from 0 to 127, as said below
- counts: int32 [128], P('temporal'), may hold values from 1 to 5, as said below
- out_weight: bfloat16 [1536, 1536], replicated, may hold values from -0.15625 to 0.15625
Outputs:
- projected: bfloat16 [16384, 1536], P(('temporal', 'ulysses'))
Inputs may be any that keep to these rules, and one draw needn't show every extreme that they name: `tile_list`: every id in row g lies within 3 of g and in the same video as g; the first entry is g itself; the first counts[g] entries are distinct; entries past counts[g] equal g. `counts`: some tile has 5 live entries.
All inputs are finite; a program needn't handle non-finite values.
Results may differ from a plain program's by a relative error of at most 0.0056.
Values may be sent and summed in bfloat16 or wider, within the bound.
No kernel may reach another device: no remote copies, remote signals or barrier semaphores. Data moves between devices by JAX's collectives and lax.ppermute only.
A program may use at most 64 MiB of HBM per device.

v0:
```python
import functools
import math

import jax
import jax.numpy as jnp
from jax import lax
from jax.experimental import pallas as pl
from jax.experimental.pallas import tpu as pltpu
from jax.sharding import PartitionSpec as P

HD = 128
TILE = 128
REACH = 3
STRIP = 256
HBM = pl.BlockSpec(memory_space=pltpu.HBM)
VMEM = pl.BlockSpec(memory_space=pltpu.VMEM)
SMEM = pl.BlockSpec(memory_space=pltpu.SMEM)
VMEM_LIMIT = 14 * 1024 * 1024
VMEM_WHOLE = 63 * 1024 * 1024


def split_heads(heads):
    sizes = []
    for share in (3 / 12, 3 / 12, 2 / 12, 2 / 12):
        size = min(max(1, round(share * heads)), heads - sum(sizes) - 1)
        if size > 0:
            sizes.append(size)
    return sizes + [heads - sum(sizes)]


def pack_kernel(groups, q_groups, cuts, *refs):
    refs = list(refs)
    cut_ref = refs.pop(0) if cuts else None
    q_ref, k_ref, v_ref = [refs.pop(0) for _ in range(3)]
    outs = [refs.pop(0) for _ in groups]
    q_outs = [refs.pop(0) for _ in q_groups]
    cut_outs = [refs.pop(0) for _ in cuts]
    k_buf, out_buf, q_buf, sems, q_sems, cut_sems = refs
    rows = k_ref.shape[0]
    jobs, q_jobs = [], []
    for out, (low, size) in zip(outs, groups):
        for h in range(size):
            at = len(jobs)
            cols = pl.ds((low + h) * HD, HD)
            jobs.append(
                (
                    pltpu.make_async_copy(k_ref.at[:, cols], k_buf.at[at], sems.at[at, 0]),
                    pltpu.make_async_copy(v_ref.at[:, cols], out_buf.at[at, 1], sems.at[at, 1]),
                    pltpu.make_async_copy(out_buf.at[at], out.at[h], sems.at[at, 2]),
                )
            )
    for out, (low, size) in zip(q_outs, q_groups):
        for h in range(size):
            at = len(q_jobs)
            cols = pl.ds((low + h) * HD, HD)
            q_jobs.append(
                (
                    pltpu.make_async_copy(q_ref.at[:, cols], q_buf.at[at], q_sems.at[at, 0]),
                    pltpu.make_async_copy(q_buf.at[at], out.at[h], q_sems.at[at, 1]),
                )
            )
    for load_k, load_v, _ in jobs:
        load_k.start()
        load_v.start()
    for load, _ in q_jobs:
        load.start()
    for at, (load_k, load_v, store) in enumerate(jobs):
        load_k.wait()
        for tile in range(rows // TILE):
            span = slice(tile * TILE, (tile + 1) * TILE)
            out_buf[at, 0, span] = k_buf[at, span].T
        load_v.wait()
        store.start()
    cut_jobs = []
    if cuts:
        size = groups[-1][1]
        for h in range(size):
            for i, (extent, out) in enumerate(zip(cuts, cut_outs)):
                part = pl.ds(pl.multiple_of(cut_ref[i] * TILE, TILE), extent * TILE)
                source = out_buf.at[len(jobs) - size + h, :, part]
                cut_jobs.append(pltpu.make_async_copy(source, out.at[h], cut_sems.at[h, i]))
                cut_jobs[-1].start()
    for load, store in q_jobs:
        load.wait()
        store.start()
    for _, _, store in jobs:
        store.wait()
    for _, store in q_jobs:
        store.wait()
    for store in cut_jobs:
        store.wait()


def pack(cut_at, queries, keys, values, groups, q_groups, cuts, limit):
    rows = keys.shape[0]
    heads = sum(size for _, size in groups)
    q_heads = sum(size for _, size in q_groups)
    last = groups[-1][1]
    shapes = [(size, 2, rows, HD) for _, size in groups] + [(size, rows, HD) for _, size in q_groups]
    shapes += [(last, 2, extent * TILE, HD) for extent in cuts]
    return pl.pallas_call(
        functools.partial(pack_kernel, groups, q_groups, cuts),
        out_shape=[jax.ShapeDtypeStruct(shape, keys.dtype) for shape in shapes],
        in_specs=[SMEM] * bool(cuts) + [HBM] * 3,
        out_specs=[HBM] * len(shapes),
        scratch_shapes=[
            pltpu.VMEM((heads, rows, HD), keys.dtype),
            pltpu.VMEM((heads, 2, rows, HD), keys.dtype),
            pltpu.VMEM((max(q_heads, 1), rows, HD), keys.dtype),
            pltpu.SemaphoreType.DMA((heads, 3)),
            pltpu.SemaphoreType.DMA((max(q_heads, 1), 2)),
            pltpu.SemaphoreType.DMA((last, max(len(cuts), 1))),
        ],
        compiler_params=pltpu.CompilerParams(vmem_limit_bytes=limit),
        cost_estimate=pl.CostEstimate(flops=0, bytes_accessed=8 * rows * heads * HD, transcendentals=0),
    )(*([cut_at] if cuts else []), queries, keys, values)


def attend_kernel(cfg, meta, q_ref, *refs):
    low, size, pieces, place_at, list_at, slots, spans, early, has_acc, final = cfg
    refs = list(refs)
    piece_refs = [refs.pop(0) for _ in range(pieces)]
    early_refs = [refs.pop(0) for _ in early or ()]
    w_ref = None if early is None else refs.pop(0)
    acc_ref = refs.pop(0) if has_acc else None
    out_ref, kv_buf = refs[:2]
    rows = q_ref.shape[1]
    tiles = rows // TILE
    att_buf, lead = out_ref, 0
    if early is not None:
        att_buf = refs[2]
        for extent, ref in zip(early, early_refs):
            att_buf[:, lead * HD : (lead + extent) * HD] = ref[...]
            lead += extent

    scale = math.log2(math.e) / math.sqrt(HD)
    zeros = jnp.zeros((TILE, HD), jnp.bfloat16)
    places, v_places, ones = [], [], []
    for tile in range(tiles):
        row = list_at + tile * (slots + 1)
        live = meta[row]
        at = [pl.multiple_of(meta[row + 1 + j] * TILE, TILE) for j in range(slots)]
        places.append(at)
        v_places.append([pl.multiple_of(jnp.where(j < live, at[j], spans), TILE) for j in range(slots)])
        ones.append([zeros + jnp.where(j < live, 1.0, 0.0).astype(jnp.bfloat16) for j in range(slots)])

    def scores(h, tile):
        k = jnp.concatenate([kv_buf[h % 2, 0, pl.ds(p, TILE)] for p in places[tile]], axis=1)
        q = q_ref[h, tile * TILE : (tile + 1) * TILE]
        return jnp.dot(q, k, preferred_element_type=jnp.float32)

    def finish(h, tile, s):
        top = jnp.max(s, axis=1, keepdims=True)
        p = jnp.exp2((s - top) * scale).astype(jnp.bfloat16)
        v = jnp.concatenate(
            [
                jnp.concatenate([kv_buf[h % 2, 1, pl.ds(at, TILE)], one], axis=1)
                for at, one in zip(v_places[tile], ones[tile])
            ],
            axis=0,
        )
        mixed = jnp.dot(p, v, preferred_element_type=jnp.float32)
        here = slice(tile * TILE, (tile + 1) * TILE)
        att_buf[here, (lead + h) * HD : (lead + h + 1) * HD] = (mixed[:, :HD] / mixed[:, HD:]).astype(jnp.bfloat16)

    def ready(h):
        for i, ref in enumerate(piece_refs):
            place = pl.ds(pl.multiple_of(meta[place_at + i] * TILE, TILE), ref.shape[2])
            for part in range(2):
                kv_buf[h % 2, part, place] = ref[h, part]
        kv_buf[h % 2, 1, spans : spans + TILE] = zeros

    jobs = [(h, tile) for h in range(size) for tile in range(tiles)]
    ready(0)
    ahead = scores(*jobs[0])
    for i, (h, tile) in enumerate(jobs):
        now = ahead
        if i + 1 < len(jobs):
            if jobs[i + 1][0] != h:
                ready(h + 1)
            ahead = scores(*jobs[i + 1])
        finish(h, tile, now)

    if early is None:
        return
    stores = []
    out_buf, out_sems = refs[3:] if final else (out_ref, None)
    for i, at in enumerate(range(0, out_buf.shape[1], STRIP)):
        here = slice(at, min(at + STRIP, out_buf.shape[1]))
        weights = w_ref[(low - lead) * HD : (low + size) * HD, here]
        part = jnp.dot(att_buf[...], weights, preferred_element_type=jnp.float32)
        if has_acc:
            part = part + acc_ref[:, here]
        out_buf[:, here] = part.astype(out_buf.dtype)
        if final:
            cols = pl.ds(at, here.stop - at)
            stores.append(pltpu.make_async_copy(out_buf.at[:, cols], out_ref.at[:, cols], out_sems.at[i]))
            stores[-1].start()
    for copy in stores:
        copy.wait()


def attend(meta, layout, queries, pieces, span, early, out_weight, acc, final):
    rows = queries.shape[1]
    low, size = span
    place_at, list_at, slots, reach = layout
    width = out_weight.shape[1]
    bf16 = jnp.bfloat16
    operands = [meta, queries, *pieces]
    scratch = [pltpu.VMEM((2, 2, reach + TILE, HD), bf16)]
    parts = None
    out_shape = jax.ShapeDtypeStruct((rows, size * HD), bf16)
    if early is not None:
        parts = tuple(part.shape[1] // HD for part in early)
        operands += [*early, out_weight]
        if acc is not None:
            operands.append(acc)
        scratch.append(pltpu.VMEM((rows, (size + sum(parts)) * HD), bf16))
        out_shape = jax.ShapeDtypeStruct((rows, width), bf16 if final else jnp.float32)
        if final:
            scratch += [pltpu.VMEM((rows, width), bf16), pltpu.SemaphoreType.DMA((-(-width // STRIP),))]
    return pl.pallas_call(
        functools.partial(
            attend_kernel, (low, size, len(pieces), place_at, list_at, slots, reach, parts, acc is not None, final)
        ),
        out_shape=out_shape,
        in_specs=[SMEM] + [VMEM] * (len(operands) - 1),
        out_specs=HBM if final else VMEM,
        scratch_shapes=scratch,
        compiler_params=pltpu.CompilerParams(vmem_limit_bytes=VMEM_LIMIT),
        cost_estimate=pl.CostEstimate(flops=0, bytes_accessed=0, transcendentals=0),
    )(*operands)


def after(array, *others):
    return lax.optimization_barrier((array, *others))[0]


def on_device(queries, keys, values, tile_list, counts, out_weight):
    rows, model = queries.shape
    tiles = rows // TILE
    groups, members = lax.axis_size("temporal"), lax.axis_size("ulysses")
    group, member = lax.axis_index("temporal"), lax.axis_index("ulysses")
    total = groups * members
    both = ("temporal", "ulysses")
    hops = -(-REACH // tiles)
    relay = members == 2 and hops == 1
    rim = min(REACH, tiles)
    cuts = [rim, tiles - rim] if relay and tiles > rim else []
    whole_at = [tiles * hops] + [tiles * i for i in range(2 * hops + 1) if i != hops]
    cut_at = [member * (tiles - rim), (1 - member) * rim]
    part_at = []
    if relay:
        whole_at = [tiles, 2 * tiles * (1 - member), 2 * tiles * member]
        part_at = [
            tiles,
            (1 - member) * (3 * tiles - rim),
            (1 - member) * 2 * tiles + member * rim,
            (1 - member) * (tiles - rim) + member * 2 * tiles,
        ]
    first = ((group * members + member) - hops) * tiles
    slots = tile_list.shape[1]
    lists = jnp.concatenate([counts[:, None], tile_list - first], axis=1)
    lists = lax.dynamic_slice_in_dim(lists, member * tiles, tiles, axis=0)
    meta = jnp.concatenate([jnp.stack([jnp.asarray(x, jnp.int32) for x in whole_at + part_at]), lists.reshape(-1)])
    cut_at = jnp.stack([jnp.asarray(x, jnp.int32) for x in cut_at])

    spans, low = [], 0
    for size in split_heads(model // HD):
        spans.append((low, size))
        low += size
    count = len(spans)
    sent = pack(None, queries, keys, values, spans[:1], [], [], VMEM_WHOLE)
    laid = pack(cut_at, queries, after(keys, *sent), values, spans, spans, cuts, VMEM_LIMIT)
    blocks, heads_of, parts = laid[:count], laid[count : 2 * count], laid[2 * count :]
    sent = [[block] for block in (*sent, *blocks[1:])]
    if parts and count > 1:
        sent[-1] = parts

    onward = [(2 * g, 2 * g + 2) for g in range(groups - 1)]
    onward += [(2 * g + 3, 2 * g + 1) for g in range(groups - 1)]
    near = []
    for i, group_sent in enumerate(sent):
        if relay:
            swap = [(0, 1), (1, 0)]
            near.append([])
            for name, block in zip(("partner", "rest"), group_sent):
                with jax.named_scope(f"{name}_{i}"):
                    near[-1].append(lax.ppermute(block, "ulysses", swap))
        else:
            near.append(
                [
                    lax.ppermute(group_sent[0], both, [(j, j - o) for j in range(total) if 0 <= j - o < total])
                    for o in range(-hops, hops + 1)
                    if o
                ]
            )

    results, acc, mid = [], None, count - 3
    for i in range(count + 1):
        if i < count:
            pieces = [blocks[i], *near[i]]
            if relay:
                gate = near[i][0] if i < 2 else after(near[i][0], results[i - 2])
                with jax.named_scope(f"onward_{i}"):
                    pieces.append(lax.ppermute(gate, both, onward))
        if i >= 1:
            j = i - 1
            final = i == count
            early = None
            if final:
                early = results[max(mid + 1, 0) :]
            elif j == mid:
                early = results[:]
            split = relay and len(sent[j]) > 1
            layout = (len(whole_at) if split else 0, meta.shape[0] - lists.size, slots, len(whole_at) * rows)
            with jax.named_scope(f"attend_{j}"):
                result = attend(meta, layout, heads_of[j], held, spans[j], early, out_weight, acc if final else None, final)
            results.append(result)
            if j == mid:
                acc = result
        held = pieces
    return results[-1]


def solution(mesh):
    return jax.shard_map(
        on_device,
        mesh=mesh,
        in_specs=(
            P(("temporal", "ulysses"), None),
            P(("temporal", "ulysses"), None),
            P(("temporal", "ulysses"), None),
            P("temporal", None),
            P("temporal"),
            P(),
        ),
        out_specs=P(("temporal", "ulysses"), None),
        check_vma=False,
    )
```

profile of v0, /device:TPU:8, one launch (start us, length us, event | category | flops | bytes accessed | tf_op | source)
XLA Modules:
  0.0 83.2 jit_solution(9936839315770944394)
XLA Ops:
  0.0 2.1 %shard_map.64 = bf16[3,2,512,128]{3,2,1,0:T(8,128)(2,1)} custom-call(bf16[512,1536]{1,0:T(8,128)(2,1)} %refs_1_.3, bf16[512,1536]{1,0:T(8,128)(2,1)} %refs_2_.2, bf16[512,1536]{1,0:T(8,128)(2,1)} %refs_3_.1), custom_call_target="tpu_custom_call" | custom-call | bytes 1572864 | tf_op jit(solution)/shard_map/pallas_call | solution.py:101
  2.1 1.6 %collective-permute-start.3 = (bf16[3,2,512,128]{3,2,1,0:T(8,128)(2,1)}, bf16[3,2,512,128]{3,2,1,0:T(8,128)(2,1)S(1)}, u32[]{:S(2)}, u32[]{:S(2)}) collective-permute-start(bf16[3,2,512,128]{3,2,1,0:T(8,128)(2,1)} %shard_map.64), channel_id=1, source_target_pairs={{0,1},{1,0},{2,3},{3,2},{4,5},{5,4},{6,7},{7,6},{8,9},{9,8},{10,11... | collective-permute-start | bytes 2359304 | tf_op jit(solution)/shard_map/partner_0/ppermute | solution.py:289
  3.7 1.4 %copy-done.1 = bf16[512,1536]{1,0:T(8,128)(2,1)S(1)} copy-done((bf16[512,1536]{1,0:T(8,128)(2,1)S(1)}, bf16[512,1536]{1,0:T(8,128)(2,1)}, u32[]{:S(2)}) %copy-start.1) | copy-done | bytes 1572888
  5.1 1.4 %copy-done.2 = bf16[512,1536]{1,0:T(8,128)(2,1)S(1)} copy-done((bf16[512,1536]{1,0:T(8,128)(2,1)S(1)}, bf16[512,1536]{1,0:T(8,128)(2,1)}, u32[]{:S(2)}) %copy-start.2) | copy-done | bytes 1572888
  6.5 1.4 %copy-done.3 = bf16[512,1536]{1,0:T(8,128)(2,1)S(1)} copy-done((bf16[512,1536]{1,0:T(8,128)(2,1)S(1)}, bf16[512,1536]{1,0:T(8,128)(2,1)}, u32[]{:S(2)}) %copy-start.3) | copy-done | bytes 1572888
  8.0 5.6 %shard_map.65 = (bf16[3,2,512,128]{3,2,1,0:T(8,128)(2,1)S(1)}, bf16[3,2,512,128]{3,2,1,0:T(8,128)(2,1)S(1)}, bf16[2,2,512,128]{3,2,1,0:T(8,128)(2,1)}, bf16[2,2,...) custom-call(s32[2]{0:T(128)S(1)} %pad_add_fusion.1.refs_0_, ...), custom_call_target="tpu_custom_call" | custom-call | bytes 6291456 | tf_op jit(solution)/shard_map/pallas_call | solution.py:101
  19.2 3.2 %collective-permute-done.3.refs_1_ = bf16[3,2,512,128]{3,2,1,0:T(8,128)(2,1)S(1)} collective-permute-done((bf16[3,2,512,128]{3,2,1,0:T(8,128)(2,1)}, bf16[3,2,512,128]{3,2,1,0:T(8,128)(2,1)S(1)}, u32[]{:S(2)}, u32[]{:S(2)}) %collective-permute-start.3) | collective-permute-done | bytes 786464 | tf_op jit(solution)/shard_map/partner_0/ppermute | solution.py:289
  22.4 1.9 %collective-permute-start.4 = (bf16[3,2,512,128]{3,2,1,0:T(8,128)(2,1)S(1)}, bf16[3,2,512,128]{3,2,1,0:T(8,128)(2,1)}, u32[]{:S(2)}, u32[]{:S(2)}) collective-permute-start(bf16[3,2,512,128]{3,2,1,0:T(8,128)(2,1)S(1)} %collective-permute-done.3.refs_1_), channel_id=1, source_target_pairs={{0,2},{2,4},{4,6},{6,8},{8,10},{10,12},{12,14},{14,16},{16,18},{18... | collective-permute-start | bytes 2359304 | tf_op jit(solution)/shard_map/onward_0/ppermute | solution.py:306
  24.3 2.0 %collective-permute-start.2 = (bf16[2,2,512,128]{3,2,1,0:T(8,128)(2,1)}, bf16[2,2,512,128]{3,2,1,0:T(8,128)(2,1)}, u32[]{:S(2)}, u32[]{:S(2)}) collective-permute-start(bf16[2,2,512,128]{3,2,1,0:T(8,128)(2,1)} %get-tuple-element.27.refs_0_), channel_id=1, source_target_pairs={{0,1},{1,0},{2,3},{3,2},{4,5},{5,4},{6,7},{7,6},{8,9},{9,8},{10,11... | collective-permute-start | bytes 1572872 | tf_op jit(solution)/shard_map/partner_2/ppermute | solution.py:289
  26.5 12.7 %collective-permute-done.6.refs_1_ = bf16[3,2,512,128]{3,2,1,0:T(8,128)(2,1)S(1)} collective-permute-done((bf16[3,2,512,128]{3,2,1,0:T(8,128)(2,1)S(1)}, bf16[3,2,512,128]{3,2,1,0:T(8,128)(2,1)S(1)}, u32[]{:S(2)}, u32[]{:S(2)}) %collective-permute-start.6) | collective-permute-done | bytes 786464 | tf_op jit(solution)/shard_map/partner_1/ppermute | solution.py:289
  39.2 1.9 %collective-permute-start.7 = (bf16[3,2,512,128]{3,2,1,0:T(8,128)(2,1)S(1)}, bf16[3,2,512,128]{3,2,1,0:T(8,128)(2,1)}, u32[]{:S(2)}, u32[]{:S(2)}) collective-permute-start(bf16[3,2,512,128]{3,2,1,0:T(8,128)(2,1)S(1)} %collective-permute-done.6.refs_1_), channel_id=1, source_target_pairs={{0,2},{2,4},{4,6},{6,8},{8,10},{10,12},{12,14},{14,16},{16,18},{18... | collective-permute-start | bytes 2359304 | tf_op jit(solution)/shard_map/onward_1/ppermute | solution.py:306
  42.4 3.2 %attend_0.1.refs_3_ = bf16[512,384]{1,0:T(8,128)(2,1)S(1)} custom-call(s32[31]{0:T(128)S(1)} %concatenate.7.meta, bf16[3,512,128]{2,1,0:T(8,128)(2,1)S(1)} %copy-done.7, bf16[3,2,512,128]{3,2,1,0:T(8,128)(2,1)S(1)} %get-tuple-element.29.refs_0_, bf16[3,2,512,128]{3,2,1,0:T(8,128)(2,1)S(1)} %collective-permute-done.3.refs_1_, ...), custom_call_target="tpu_custom_call" | custom-call | tf_op jit(solution)/shard_map/attend_0/pallas_call | solution.py:222
  45.7 4.9 %collective-permute-done.2.refs_1_ = bf16[2,2,512,128]{3,2,1,0:T(8,128)(2,1)} collective-permute-done((bf16[2,2,512,128]{3,2,1,0:T(8,128)(2,1)}, bf16[2,2,512,128]{3,2,1,0:T(8,128)(2,1)}, u32[]{:S(2)}, u32[]{:S(2)}) %collective-permute-start.2) | collective-permute-done | bytes 524320 | tf_op jit(solution)/shard_map/partner_2/ppermute | solution.py:289
  50.6 1.9 %collective-permute-start.5 = (bf16[2,2,512,128]{3,2,1,0:T(8,128)(2,1)}, bf16[2,2,512,128]{3,2,1,0:T(8,128)(2,1)S(1)}, u32[]{:S(2)}, u32[]{:S(2)}) collective-permute-start(bf16[2,2,512,128]{3,2,1,0:T(8,128)(2,1)} %collective-permute-done.2.refs_1_), channel_id=1, source_target_pairs={{0,2},{2,4},{4,6},{6,8},{8,10},{10,12},{12,14},{14,16},{16,18},{18... | collective-permute-start | bytes 1572872 | tf_op jit(solution)/shard_map/onward_2/ppermute | solution.py:306
  52.5 2.0 %collective-permute-start = (bf16[2,2,384,128]{3,2,1,0:T(8,128)(2,1)}, bf16[2,2,384,128]{3,2,1,0:T(8,128)(2,1)S(1)}, u32[]{:S(2)}, u32[]{:S(2)}) collective-permute-start(bf16[2,2,384,128]{3,2,1,0:T(8,128)(2,1)} %copy-done.14), channel_id=1, source_target_pairs={{0,1},{1,0},{2,3},{3,2},{4,5},{5,4},{6,7},{7,6},{8,9},{9,8},{10,11... | collective-permute-start | bytes 1179656 | tf_op jit(solution)/shard_map/partner_4/ppermute | solution.py:289
  54.5 3.1 %attend_1.1.refs_4_ = bf16[512,384]{1,0:T(8,128)(2,1)S(1)} custom-call(s32[31]{0:T(128)S(1)} %concatenate.7.meta, bf16[3,512,128]{2,1,0:T(8,128)(2,1)S(1)} %get-tuple-element.31.q_ref, bf16[3,2,512,128]{3,2,1,0:T(8,128)(2,1)S(1)} %get-tuple-element.32.refs_0_, bf16[3,2,512,128]{3,2,1,0:T(8,128)(2,1)S(1)} %collective-permute-done.6.refs_1_, ...), custom_call_target="tpu_custom_call" | custom-call | tf_op jit(solution)/shard_map/attend_1/pallas_call | solution.py:222
  57.6 4.2 %collective-permute-done.9.refs_1_ = bf16[2,2,512,128]{3,2,1,0:T(8,128)(2,1)} collective-permute-done((bf16[2,2,512,128]{3,2,1,0:T(8,128)(2,1)}, bf16[2,2,512,128]{3,2,1,0:T(8,128)(2,1)}, u32[]{:S(2)}, u32[]{:S(2)}) %collective-permute-start.9) | collective-permute-done | bytes 524320 | tf_op jit(solution)/shard_map/partner_3/ppermute | solution.py:289
  61.8 1.9 %collective-permute-start.10 = (bf16[2,2,512,128]{3,2,1,0:T(8,128)(2,1)}, bf16[2,2,512,128]{3,2,1,0:T(8,128)(2,1)S(1)}, u32[]{:S(2)}, u32[]{:S(2)}) collective-permute-start(bf16[2,2,512,128]{3,2,1,0:T(8,128)(2,1)} %collective-permute-done.9.refs_1_), channel_id=1, source_target_pairs={{0,2},{2,4},{4,6},{6,8},{8,10},{10,12},{12,14},{14,16},{16,18},{18... | collective-permute-start | bytes 1572872 | tf_op jit(solution)/shard_map/onward_3/ppermute | solution.py:306
  63.8 4.3 %attend_2.1.refs_6_ = f32[512,1536]{1,0:T(8,128)S(1)} custom-call(s32[31]{0:T(128)S(1)} %concatenate.7.meta, bf16[2,512,128]{2,1,0:T(8,128)(2,1)S(1)} %copy-done.13, bf16[2,2,512,128]{3,2,1,0:T(8,128)(2,1)} %get-tuple-element.27.refs_0_, bf16[2,2,512,128]{3,2,1,0:T(8,128)(2,1)} %collective-permute-done.2.refs_1_, ...), custom_call_target="tpu_custom_call" | custom-call | tf_op jit(solution)/shard_map/attend_2/pallas_call | solution.py:222
  69.4 2.6 %collective-permute-start.8 = (bf16[2,2,384,128]{3,2,1,0:T(8,128)(2,1)S(1)}, bf16[2,2,384,128]{3,2,1,0:T(8,128)(2,1)S(1)}, u32[]{:S(2)}, u32[]{:S(2)}) collective-permute-start(bf16[2,2,384,128]{3,2,1,0:T(8,128)(2,1)S(1)} %collective-permute-done.refs_1_), channel_id=1, source_target_pairs={{0,2},{2,4},{4,6},{6,8},{8,10},{10,12},{12,14},{14,16},{16,18},{18... | collective-permute-start | bytes 1179656 | tf_op jit(solution)/shard_map/onward_4/ppermute | solution.py:306
  72.0 1.9 %collective-permute-start.1 = (bf16[2,2,128,128]{3,2,1,0:T(8,128)(2,1)S(1)}, bf16[2,2,128,128]{3,2,1,0:T(8,128)(2,1)S(1)}, u32[]{:S(2)}, u32[]{:S(2)}) collective-permute-start(bf16[2,2,128,128]{3,2,1,0:T(8,128)(2,1)S(1)} %copy-done.16), channel_id=1, source_target_pairs={{0,1},{1,0},{2,3},{3,2},{4,5},{5,4},{6,7},{7,6},{8,9},{9,8},{10,11... | collective-permute-start | bytes 393224 | tf_op jit(solution)/shard_map/rest_4/ppermute | solution.py:289
  73.9 2.6 %attend_3.1.refs_4_ = bf16[512,256]{1,0:T(8,128)(2,1)S(1)} custom-call(s32[31]{0:T(128)S(1)} %concatenate.7.meta, bf16[2,512,128]{2,1,0:T(8,128)(2,1)S(1)} %copy-done.11, bf16[2,2,512,128]{3,2,1,0:T(8,128)(2,1)} %get-tuple-element.35.refs_0_, bf16[2,2,512,128]{3,2,1,0:T(8,128)(2,1)} %collective-permute-done.9.refs_1_, ...), custom_call_target="tpu_custom_call" | custom-call | tf_op jit(solution)/shard_map/attend_3/pallas_call | solution.py:222
  76.5 1.8 %collective-permute-done.1.refs_2_ = bf16[2,2,128,128]{3,2,1,0:T(8,128)(2,1)S(1)} collective-permute-done((bf16[2,2,128,128]{3,2,1,0:T(8,128)(2,1)S(1)}, bf16[2,2,128,128]{3,2,1,0:T(8,128)(2,1)S(1)}, u32[]{:S(2)}, u32[]{:S(2)}) %collective-permute-start.1) | collective-permute-done | bytes 131104 | tf_op jit(solution)/shard_map/rest_4/ppermute | solution.py:289
  79.4 3.7 %attend_4.1 = bf16[512,1536]{1,0:T(8,128)(2,1)} custom-call(s32[31]{0:T(128)S(1)} %concatenate.7.meta, bf16[2,512,128]{2,1,0:T(8,128)(2,1)S(1)} %copy-done.9, bf16[2,2,512,128]{3,2,1,0:T(8,128)(2,1)S(1)} %copy-done.5, bf16[2,2,384,128]{3,2,1,0:T(8,128)(2,1)S(1)} %collective-permute-done.refs_1_, bf16[2,2,128,128]{3,2,1,0:T(8,128)(2,1)S(1)} %collective-permute-done.1.refs_2_, ...), custom_call_target="tpu_custom_call" | custom-call | tf_op jit(solution)/shard_map/attend_4/pallas_call | solution.py:222
  (50 shorter events, 9.6 us)
Async XLA Ops:
  2.1 20.3 %collective-permute-start.3 = (bf16[3,2,512,128]{3,2,1,0:T(8,128)(2,1)}, bf16[3,2,512,128]{3,2,1,0:T(8,128)(2,1)S(1)}, u32[]{:S(2)}, u32[]{:S(2)}) collective-permute-start(bf16[3,2,512,128]{3,2,1,0:T(8,128)(2,1)} %shard_map.64), channel_id=1, source_target_pairs={{0,1},{1,0},{2,3},{3,2},{4,5},{5,4},{6,7},{7,6},{8,9},{9,8},{10,11... | collective-permute-start | bytes 2359304 | tf_op jit(solution)/shard_map/partner_0/ppermute | solution.py:289
  3.7 1.4 %copy-start.1 = (bf16[512,1536]{1,0:T(8,128)(2,1)S(1)}, bf16[512,1536]{1,0:T(8,128)(2,1)}, u32[]{:S(2)}) copy-start(bf16[512,1536]{1,0:T(8,128)(2,1)} %refs_1_.3) | copy-start | bytes 4718596
  5.1 1.4 %copy-start.2 = (bf16[512,1536]{1,0:T(8,128)(2,1)S(1)}, bf16[512,1536]{1,0:T(8,128)(2,1)}, u32[]{:S(2)}) copy-start(bf16[512,1536]{1,0:T(8,128)(2,1)} %refs_2_.2) | copy-start | bytes 4718596
  6.5 1.4 %copy-start.3 = (bf16[512,1536]{1,0:T(8,128)(2,1)S(1)}, bf16[512,1536]{1,0:T(8,128)(2,1)}, u32[]{:S(2)}) copy-start(bf16[512,1536]{1,0:T(8,128)(2,1)} %refs_3_.1) | copy-start | bytes 4718596
  8.0 18.5 %copy-start.18 = (s32[8]{0:T(128)S(1)}, s32[8]{0:T(128)}, u32[]{:S(2)}) copy-start(s32[8]{0:T(128)} %param.10) | copy-start | bytes 100
  8.0 33.2 %copy-start.17 = (s32[8,5]{1,0:T(8,128)S(1)}, s32[8,5]{1,0:T(8,128)}, u32[]{:S(2)}) copy-start(s32[8,5]{1,0:T(8,128)} %param.9) | copy-start | bytes 484
  13.6 0.8 copy-start.4
  18.7 20.5 %collective-permute-start.6 = (bf16[3,2,512,128]{3,2,1,0:T(8,128)(2,1)S(1)}, bf16[3,2,512,128]{3,2,1,0:T(8,128)(2,1)S(1)}, u32[]{:S(2)}, u32[]{:S(2)}) collective-permute-start(bf16[3,2,512,128]{3,2,1,0:T(8,128)(2,1)S(1)} %get-tuple-element.32.refs_0_), channel_id=1, source_target_pairs={{0,1},{1,0},{2,3},{3,2},{4,5},{5,4},{6,7},{7,6},{8,9},{9,8},{10,11... | collective-permute-start | bytes 2359304 | tf_op jit(solution)/shard_map/partner_1/ppermute | solution.py:289
  22.4 19.1 %collective-permute-start.4 = (bf16[3,2,512,128]{3,2,1,0:T(8,128)(2,1)S(1)}, bf16[3,2,512,128]{3,2,1,0:T(8,128)(2,1)}, u32[]{:S(2)}, u32[]{:S(2)}) collective-permute-start(bf16[3,2,512,128]{3,2,1,0:T(8,128)(2,1)S(1)} %collective-permute-done.3.refs_1_), channel_id=1, source_target_pairs={{0,2},{2,4},{4,6},{6,8},{8,10},{10,12},{12,14},{14,16},{16,18},{18... | collective-permute-start | bytes 2359304 | tf_op jit(solution)/shard_map/onward_0/ppermute | solution.py:306
  24.3 26.3 %collective-permute-start.2 = (bf16[2,2,512,128]{3,2,1,0:T(8,128)(2,1)}, bf16[2,2,512,128]{3,2,1,0:T(8,128)(2,1)}, u32[]{:S(2)}, u32[]{:S(2)}) collective-permute-start(bf16[2,2,512,128]{3,2,1,0:T(8,128)(2,1)} %get-tuple-element.27.refs_0_), channel_id=1, source_target_pairs={{0,1},{1,0},{2,3},{3,2},{4,5},{5,4},{6,7},{7,6},{8,9},{9,8},{10,11... | collective-permute-start | bytes 1572872 | tf_op jit(solution)/shard_map/partner_2/ppermute | solution.py:289
  26.3 35.5 %collective-permute-start.9 = (bf16[2,2,512,128]{3,2,1,0:T(8,128)(2,1)}, bf16[2,2,512,128]{3,2,1,0:T(8,128)(2,1)}, u32[]{:S(2)}, u32[]{:S(2)}) collective-permute-start(bf16[2,2,512,128]{3,2,1,0:T(8,128)(2,1)} %get-tuple-element.35.refs_0_), channel_id=1, source_target_pairs={{0,1},{1,0},{2,3},{3,2},{4,5},{5,4},{6,7},{7,6},{8,9},{9,8},{10,11... | collective-permute-start | bytes 1572872 | tf_op jit(solution)/shard_map/partner_3/ppermute | solution.py:289
  39.2 15.2 %collective-permute-start.7 = (bf16[3,2,512,128]{3,2,1,0:T(8,128)(2,1)S(1)}, bf16[3,2,512,128]{3,2,1,0:T(8,128)(2,1)}, u32[]{:S(2)}, u32[]{:S(2)}) collective-permute-start(bf16[3,2,512,128]{3,2,1,0:T(8,128)(2,1)S(1)} %collective-permute-done.6.refs_1_), channel_id=1, source_target_pairs={{0,2},{2,4},{4,6},{6,8},{8,10},{10,12},{12,14},{14,16},{16,18},{18... | collective-permute-start | bytes 2359304 | tf_op jit(solution)/shard_map/onward_1/ppermute | solution.py:306
  41.4 1.0 %copy-start.7 = (bf16[3,512,128]{2,1,0:T(8,128)(2,1)S(1)}, bf16[3,512,128]{2,1,0:T(8,128)(2,1)}, u32[]{:S(2)}) copy-start(bf16[3,512,128]{2,1,0:T(8,128)(2,1)} %copy-done.6) | copy-start | bytes 1179652
  42.4 21.3 %copy-start = (bf16[1536,1536]{1,0:T(8,128)(2,1)S(1)}, bf16[1536,1536]{1,0:T(8,128)(2,1)}, u32[]{:S(2)}) copy-start(bf16[1536,1536]{1,0:T(8,128)(2,1)} %refs_5_.3) | copy-start | bytes 14155780
  50.6 13.2 %collective-permute-start.5 = (bf16[2,2,512,128]{3,2,1,0:T(8,128)(2,1)}, bf16[2,2,512,128]{3,2,1,0:T(8,128)(2,1)S(1)}, u32[]{:S(2)}, u32[]{:S(2)}) collective-permute-start(bf16[2,2,512,128]{3,2,1,0:T(8,128)(2,1)} %collective-permute-done.2.refs_1_), channel_id=1, source_target_pairs={{0,2},{2,4},{4,6},{6,8},{8,10},{10,12},{12,14},{14,16},{16,18},{18... | collective-permute-start | bytes 1572872 | tf_op jit(solution)/shard_map/onward_2/ppermute | solution.py:306
  52.5 16.9 %collective-permute-start = (bf16[2,2,384,128]{3,2,1,0:T(8,128)(2,1)}, bf16[2,2,384,128]{3,2,1,0:T(8,128)(2,1)S(1)}, u32[]{:S(2)}, u32[]{:S(2)}) collective-permute-start(bf16[2,2,384,128]{3,2,1,0:T(8,128)(2,1)} %copy-done.14), channel_id=1, source_target_pairs={{0,1},{1,0},{2,3},{3,2},{4,5},{5,4},{6,7},{7,6},{8,9},{9,8},{10,11... | collective-permute-start | bytes 1179656 | tf_op jit(solution)/shard_map/partner_4/ppermute | solution.py:289
  54.5 9.3 %copy-start.13 = (bf16[2,512,128]{2,1,0:T(8,128)(2,1)S(1)}, bf16[2,512,128]{2,1,0:T(8,128)(2,1)}, u32[]{:S(2)}) copy-start(bf16[2,512,128]{2,1,0:T(8,128)(2,1)} %copy-done.12) | copy-start | bytes 786436
  61.8 12.0 %collective-permute-start.10 = (bf16[2,2,512,128]{3,2,1,0:T(8,128)(2,1)}, bf16[2,2,512,128]{3,2,1,0:T(8,128)(2,1)S(1)}, u32[]{:S(2)}, u32[]{:S(2)}) collective-permute-start(bf16[2,2,512,128]{3,2,1,0:T(8,128)(2,1)} %collective-permute-done.9.refs_1_), channel_id=1, source_target_pairs={{0,2},{2,4},{4,6},{6,8},{8,10},{10,12},{12,14},{14,16},{16,18},{18... | collective-permute-start | bytes 1572872 | tf_op jit(solution)/shard_map/onward_3/ppermute | solution.py:306
  63.8 8.2 %copy-start.16 = (bf16[2,2,128,128]{3,2,1,0:T(8,128)(2,1)S(1)}, bf16[2,2,128,128]{3,2,1,0:T(8,128)(2,1)}, u32[]{:S(2)}) copy-start(bf16[2,2,128,128]{3,2,1,0:T(8,128)(2,1)} %copy-done.15) | copy-start | bytes 393220
  63.8 10.1 %copy-start.11 = (bf16[2,512,128]{2,1,0:T(8,128)(2,1)S(1)}, bf16[2,512,128]{2,1,0:T(8,128)(2,1)}, u32[]{:S(2)}) copy-start(bf16[2,512,128]{2,1,0:T(8,128)(2,1)} %copy-done.10) | copy-start | bytes 786436
  68.1 11.3 %copy-start.5 = (bf16[2,2,512,128]{3,2,1,0:T(8,128)(2,1)S(1)}, bf16[2,2,512,128]{3,2,1,0:T(8,128)(2,1)}, u32[]{:S(2)}) copy-start(bf16[2,2,512,128]{3,2,1,0:T(8,128)(2,1)} %copy-done.4) | copy-start | bytes 1572868
  68.1 11.3 %copy-start.9 = (bf16[2,512,128]{2,1,0:T(8,128)(2,1)S(1)}, bf16[2,512,128]{2,1,0:T(8,128)(2,1)}, u32[]{:S(2)}) copy-start(bf16[2,512,128]{2,1,0:T(8,128)(2,1)} %copy-done.8) | copy-start | bytes 786436
  69.4 10.0 %collective-permute-start.8 = (bf16[2,2,384,128]{3,2,1,0:T(8,128)(2,1)S(1)}, bf16[2,2,384,128]{3,2,1,0:T(8,128)(2,1)S(1)}, u32[]{:S(2)}, u32[]{:S(2)}) collective-permute-start(bf16[2,2,384,128]{3,2,1,0:T(8,128)(2,1)S(1)} %collective-permute-done.refs_1_), channel_id=1, source_target_pairs={{0,2},{2,4},{4,6},{6,8},{8,10},{10,12},{12,14},{14,16},{16,18},{18... | collective-permute-start | bytes 1179656 | tf_op jit(solution)/shard_map/onward_4/ppermute | solution.py:306
  72.0 6.3 %collective-permute-start.1 = (bf16[2,2,128,128]{3,2,1,0:T(8,128)(2,1)S(1)}, bf16[2,2,128,128]{3,2,1,0:T(8,128)(2,1)S(1)}, u32[]{:S(2)}, u32[]{:S(2)}) collective-permute-start(bf16[2,2,128,128]{3,2,1,0:T(8,128)(2,1)S(1)} %copy-done.16), channel_id=1, source_target_pairs={{0,1},{1,0},{2,3},{3,2},{4,5},{5,4},{6,7},{7,6},{8,9},{9,8},{10,11... | collective-permute-start | bytes 393224 | tf_op jit(solution)/shard_map/rest_4/ppermute | solution.py:289
  (6 other events, 4.3 us)
where the time goes:
time: 84 us; the launch traced here: 83.2 us
  waiting for transfers between devices  29.2 us (35%)
  Pallas kernels  24.7 us (29%)
  starting transfers between devices  18.2 us (22%)
  local copies, waits for them, and re-layouts  10.6 us (13%)
    ppermute x6, waiting for transfers between devices, on_device(): near[-1].append(lax.ppermute(block, 'ulysses', swap))  28.1 us
    pallas_call x5, Pallas kernels, attend(): pl.pallas_call(functools.partial(attend_kernel, (low, size, len(pieces),...  17 us
    unnamed x38, local copies, waits for them, and re-layouts  10.4 us
    ppermute x5, starting transfers between devices, on_device(): pieces.append(lax.ppermute(gate, both, onward))  10.2 us
    ppermute x6, starting transfers between devices, on_device(): near[-1].append(lax.ppermute(block, 'ulysses', swap))  8.02 us
    pallas_call x2, Pallas kernels, pack(): pl.pallas_call(functools.partial(pack_kernel, groups, q_groups, cuts), ou...  7.7 us
  transfers between devices with their start and end apart: 11, of which 7 were waited for; matrix products, arithmetic and copies ran while one was open for 0% of the time, Pallas kernels for 23%

commit v1 on v0

--- a/solution.py
+++ b/solution.py
@@ -21,7 +21,7 @@
 
 def split_heads(heads):
     sizes = []
-    for share in (3 / 12, 3 / 12, 2 / 12, 2 / 12):
+    for share in (4 / 12, 3 / 12, 2 / 12, 2 / 12):
         size = min(max(1, round(share * heads)), heads - sum(sizes) - 1)
         if size > 0:
             sizes.append(size)
@@ -72,14 +72,12 @@
         load_v.wait()
         store.start()
     cut_jobs = []
-    if cuts:
-        size = groups[-1][1]
+    for (start, size, which, extent), out in zip(cuts, cut_outs):
+        part = pl.ds(pl.multiple_of(cut_ref[which] * TILE, TILE), extent * TILE)
         for h in range(size):
-            for i, (extent, out) in enumerate(zip(cuts, cut_outs)):
-                part = pl.ds(pl.multiple_of(cut_ref[i] * TILE, TILE), extent * TILE)
-                source = out_buf.at[len(jobs) - size + h, :, part]
-                cut_jobs.append(pltpu.make_async_copy(source, out.at[h], cut_sems.at[h, i]))
-                cut_jobs[-1].start()
+            source = out_buf.at[start - groups[0][0] + h, :, part]
+            cut_jobs.append(pltpu.make_async_copy(source, out.at[h], cut_sems.at[len(cut_jobs)]))
+            cut_jobs[-1].start()
     for load, store in q_jobs:
         load.wait()
         store.start()
@@ -95,9 +93,8 @@
     rows = keys.shape[0]
     heads = sum(size for _, size in groups)
     q_heads = sum(size for _, size in q_groups)
-    last = groups[-1][1]
     shapes = [(size, 2, rows, HD) for _, size in groups] + [(size, rows, HD) for _, size in q_groups]
-    shapes += [(last, 2, extent * TILE, HD) for extent in cuts]
+    shapes += [(size, 2, extent * TILE, HD) for _, size, _, extent in cuts]
     return pl.pallas_call(
         functools.partial(pack_kernel, groups, q_groups, cuts),
         out_shape=[jax.ShapeDtypeStruct(shape, keys.dtype) for shape in shapes],
@@ -109,7 +106,7 @@
             pltpu.VMEM((max(q_heads, 1), rows, HD), keys.dtype),
             pltpu.SemaphoreType.DMA((heads, 3)),
             pltpu.SemaphoreType.DMA((max(q_heads, 1), 2)),
-            pltpu.SemaphoreType.DMA((last, max(len(cuts), 1))),
+            pltpu.SemaphoreType.DMA((max(sum(size for _, size, _, _ in cuts), 1),)),
         ],
         compiler_params=pltpu.CompilerParams(vmem_limit_bytes=limit),
         cost_estimate=pl.CostEstimate(flops=0, bytes_accessed=8 * rows * heads * HD, transcendentals=0),
@@ -117,9 +114,9 @@
 
 
 def attend_kernel(cfg, meta, q_ref, *refs):
-    low, size, pieces, place_at, list_at, slots, spans, early, has_acc, final = cfg
+    low, size, shifts, place_at, list_at, slots, spans, early, has_acc, final = cfg
     refs = list(refs)
-    piece_refs = [refs.pop(0) for _ in range(pieces)]
+    piece_refs = [refs.pop(0) for _ in shifts]
     early_refs = [refs.pop(0) for _ in early or ()]
     w_ref = None if early is None else refs.pop(0)
     acc_ref = refs.pop(0) if has_acc else None
@@ -167,7 +164,7 @@
         for i, ref in enumerate(piece_refs):
             place = pl.ds(pl.multiple_of(meta[place_at + i] * TILE, TILE), ref.shape[2])
             for part in range(2):
-                kv_buf[h % 2, part, place] = ref[h, part]
+                kv_buf[h % 2, part, place] = ref[h + shifts[i], part]
         kv_buf[h % 2, 1, spans : spans + TILE] = zeros
 
     jobs = [(h, tile) for h in range(size) for tile in range(tiles)]
@@ -200,7 +197,7 @@
         copy.wait()
 
 
-def attend(meta, layout, queries, pieces, span, early, out_weight, acc, final):
+def attend(meta, layout, queries, pieces, shifts, span, early, out_weight, acc, final):
     rows = queries.shape[1]
     low, size = span
     place_at, list_at, slots, reach = layout
@@ -221,7 +218,7 @@
             scratch += [pltpu.VMEM((rows, width), bf16), pltpu.SemaphoreType.DMA((-(-width // STRIP),))]
     return pl.pallas_call(
         functools.partial(
-            attend_kernel, (low, size, len(pieces), place_at, list_at, slots, reach, parts, acc is not None, final)
+            attend_kernel, (low, size, shifts, place_at, list_at, slots, reach, parts, acc is not None, final)
         ),
         out_shape=out_shape,
         in_specs=[SMEM] + [VMEM] * (len(operands) - 1),
@@ -246,7 +243,6 @@
     hops = -(-REACH // tiles)
     relay = members == 2 and hops == 1
     rim = min(REACH, tiles)
-    cuts = [rim, tiles - rim] if relay and tiles > rim else []
     whole_at = [tiles * hops] + [tiles * i for i in range(2 * hops + 1) if i != hops]
     cut_at = [member * (tiles - rim), (1 - member) * rim]
     part_at = []
@@ -271,26 +267,26 @@
         low += size
     count = len(spans)
     sent = pack(None, queries, keys, values, spans[:1], [], [], VMEM_WHOLE)
+    split = max(1, count - 2) if relay and tiles > rim else count
+    cuts = [(low, size, 0, rim) for low, size in spans[split:]]
+    if cuts:
+        rest_low = spans[split][0]
+        cuts.append((rest_low, model // HD - rest_low, 1, tiles - rim))
     laid = pack(cut_at, queries, after(keys, *sent), values, spans, spans, cuts, VMEM_LIMIT)
     blocks, heads_of, parts = laid[:count], laid[count : 2 * count], laid[2 * count :]
-    sent = [[block] for block in (*sent, *blocks[1:])]
-    if parts and count > 1:
-        sent[-1] = parts
+    sent = [*sent, *blocks[1:split], *parts]
 
     onward = [(2 * g, 2 * g + 2) for g in range(groups - 1)]
     onward += [(2 * g + 3, 2 * g + 1) for g in range(groups - 1)]
     near = []
-    for i, group_sent in enumerate(sent):
+    for i, block in enumerate(sent):
         if relay:
-            swap = [(0, 1), (1, 0)]
-            near.append([])
-            for name, block in zip(("partner", "rest"), group_sent):
-                with jax.named_scope(f"{name}_{i}"):
-                    near[-1].append(lax.ppermute(block, "ulysses", swap))
+            with jax.named_scope(f"partner_{i}" if i < count else f"rest_{i}"):
+                near.append([lax.ppermute(block, "ulysses", [(0, 1), (1, 0)])])
         else:
             near.append(
                 [
-                    lax.ppermute(group_sent[0], both, [(j, j - o) for j in range(total) if 0 <= j - o < total])
+                    lax.ppermute(block, both, [(j, j - o) for j in range(total) if 0 <= j - o < total])
                     for o in range(-hops, hops + 1)
                     if o
                 ]
@@ -300,10 +296,15 @@
     for i in range(count + 1):
         if i < count:
             pieces = [blocks[i], *near[i]]
+            shifts = [0] * len(pieces)
+            if i >= split:
+                pieces += near[count]
+                shifts.append(spans[i][0] - rest_low)
             if relay:
                 gate = near[i][0] if i < 2 else after(near[i][0], results[i - 2])
                 with jax.named_scope(f"onward_{i}"):
                     pieces.append(lax.ppermute(gate, both, onward))
+                shifts.append(0)
         if i >= 1:
             j = i - 1
             final = i == count
@@ -312,14 +313,13 @@
                 early = results[max(mid + 1, 0) :]
             elif j == mid:
                 early = results[:]
-            split = relay and len(sent[j]) > 1
-            layout = (len(whole_at) if split else 0, meta.shape[0] - lists.size, slots, len(whole_at) * rows)
+            layout = (len(whole_at) if j >= split else 0, meta.shape[0] - lists.size, slots, len(whole_at) * rows)
             with jax.named_scope(f"attend_{j}"):
-                result = attend(meta, layout, heads_of[j], held, spans[j], early, out_weight, acc if final else None, final)
+                result = attend(meta, layout, heads_of[j], *held, spans[j], early, out_weight, acc if final else None, final)
             results.append(result)
             if j == mid:
                 acc = result
-        held = pieces
+        held = pieces, tuple(shifts)
     return results[-1]
 
 

time: 84 us -> 87.2 us (1.038)
  local copies, waits for them, and re-layouts: 10.6 us -> 15 us
  waiting for transfers between devices: 29.2 us -> 27.6 us
  starting transfers between devices: 18.2 us -> 19.6 us
    unnamed x38 -> x50, local copies, waits for them, and re-layouts: 10.4 us -> 14.8 us
    ppermute x6, waiting for transfers between devices: 28.1 us -> 23.8 us  [on_device(): near.append([lax.ppermute(block, 'ulysses', [(0, 1), (1, 0)])])]
    ppermute x5, waiting for transfers between devices: 1.14 us -> 3.8 us  [on_device(): pieces.append(lax.ppermute(gate, both, onward))]
    ppermute x6, starting transfers between devices: 8.02 us -> 9.49 us  [on_device(): near.append([lax.ppermute(block, 'ulysses', [(0, 1), (1, 0)])])]
  transfers between devices with their start and end apart: 11 -> 11, of which waited for: 7 -> 4; matrix products, arithmetic and copies ran while one was open for 0% -> 0% of each run, Pallas kernels for 23% -> 22%
where the time goes in v1:
time: 87.2 us; the launch traced here: 86.7 us
  waiting for transfers between devices  27.6 us (32%)
  Pallas kernels  24 us (28%)
  starting transfers between devices  19.6 us (22%)
  local copies, waits for them, and re-layouts  15 us (17%)
    ppermute x6, waiting for transfers between devices, on_device(): near.append([lax.ppermute(block, 'ulysses', [(0, 1), (1, 0)])])  23.8 us
    pallas_call x5, Pallas kernels, attend(): pl.pallas_call(functools.partial(attend_kernel, (low, size, shifts, place...  16.2 us
    unnamed x50, local copies, waits for them, and re-layouts  14.8 us
    ppermute x5, starting transfers between devices, on_device(): pieces.append(lax.ppermute(gate, both, onward))  10.1 us
    ppermute x6, starting transfers between devices, on_device(): near.append([lax.ppermute(block, 'ulysses', [(0, 1), (1, 0)])])  9.49 us
    pallas_call x2, Pallas kernels, pack(): pl.pallas_call(functools.partial(pack_kernel, groups, q_groups, cuts), ou...  7.77 us
    ppermute x5, waiting for transfers between devices, on_device(): pieces.append(lax.ppermute(gate, both, onward))  3.8 us
  transfers between devices with their start and end apart: 11, of which 4 were waited for; matrix products, arithmetic and copies ran while one was open for 0% of the time, Pallas kernels for 22%

profile of v1, /device:TPU:8, one launch (start us, length us, event | category | flops | bytes accessed | tf_op | source)
XLA Modules:
  0.0 86.7 jit_solution(6798124356197289970)
XLA Ops:
  0.0 2.2 %shard_map.64 = bf16[4,2,512,128]{3,2,1,0:T(8,128)(2,1)} custom-call(bf16[512,1536]{1,0:T(8,128)(2,1)} %refs_1_.3, bf16[512,1536]{1,0:T(8,128)(2,1)} %refs_2_.2, bf16[512,1536]{1,0:T(8,128)(2,1)} %refs_3_.1), custom_call_target="tpu_custom_call" | custom-call | bytes 2097152 | tf_op jit(solution)/shard_map/pallas_call | solution.py:98
  2.2 1.6 %collective-permute-start.3 = (bf16[4,2,512,128]{3,2,1,0:T(8,128)(2,1)}, bf16[4,2,512,128]{3,2,1,0:T(8,128)(2,1)S(1)}, u32[]{:S(2)}, u32[]{:S(2)}) collective-permute-start(bf16[4,2,512,128]{3,2,1,0:T(8,128)(2,1)} %shard_map.64), channel_id=1, source_target_pairs={{0,1},{1,0},{2,3},{3,2},{4,5},{5,4},{6,7},{7,6},{8,9},{9,8},{10,11... | collective-permute-start | bytes 3145736 | tf_op jit(solution)/shard_map/partner_0/ppermute | solution.py:285
  3.8 1.4 %copy-done.1 = bf16[512,1536]{1,0:T(8,128)(2,1)S(1)} copy-done((bf16[512,1536]{1,0:T(8,128)(2,1)S(1)}, bf16[512,1536]{1,0:T(8,128)(2,1)}, u32[]{:S(2)}) %copy-start.1) | copy-done | bytes 1572888
  5.2 1.4 %copy-done.2 = bf16[512,1536]{1,0:T(8,128)(2,1)S(1)} copy-done((bf16[512,1536]{1,0:T(8,128)(2,1)S(1)}, bf16[512,1536]{1,0:T(8,128)(2,1)}, u32[]{:S(2)}) %copy-start.2) | copy-done | bytes 1572888
  6.6 1.4 %copy-done.3 = bf16[512,1536]{1,0:T(8,128)(2,1)S(1)} copy-done((bf16[512,1536]{1,0:T(8,128)(2,1)S(1)}, bf16[512,1536]{1,0:T(8,128)(2,1)}, u32[]{:S(2)}) %copy-start.3) | copy-done | bytes 1572888
  8.1 5.6 %shard_map.65 = (bf16[4,2,512,128]{3,2,1,0:T(8,128)(2,1)S(1)}, bf16[3,2,512,128]{3,2,1,0:T(8,128)(2,1)S(1)}, bf16[2,2,512,128]{3,2,1,0:T(8,128)(2,1)}, bf16[2,2,...) custom-call(s32[2]{0:T(128)S(1)} %pad_add_fusion.1.refs_0_, ...), custom_call_target="tpu_custom_call" | custom-call | bytes 6291456 | tf_op jit(solution)/shard_map/pallas_call | solution.py:98
  21.5 7.0 %collective-permute-done.3.refs_1_ = bf16[4,2,512,128]{3,2,1,0:T(8,128)(2,1)S(1)} collective-permute-done((bf16[4,2,512,128]{3,2,1,0:T(8,128)(2,1)}, bf16[4,2,512,128]{3,2,1,0:T(8,128)(2,1)S(1)}, u32[]{:S(2)}, u32[]{:S(2)}) %collective-permute-start.3) | collective-permute-done | bytes 1048608 | tf_op jit(solution)/shard_map/partner_0/ppermute | solution.py:285
  28.5 1.9 %collective-permute-start.4 = (bf16[4,2,512,128]{3,2,1,0:T(8,128)(2,1)S(1)}, bf16[4,2,512,128]{3,2,1,0:T(8,128)(2,1)S(1)}, u32[]{:S(2)}, u32[]{:S(2)}) collective-permute-start(bf16[4,2,512,128]{3,2,1,0:T(8,128)(2,1)S(1)} %collective-permute-done.3.refs_1_), channel_id=1, source_target_pairs={{0,2},{2,4},{4,6},{6,8},{8,10},{10,12},{12,14},{14,16},{16,18},{18... | collective-permute-start | bytes 3145736 | tf_op jit(solution)/shard_map/onward_0/ppermute | solution.py:306
  30.4 1.6 %collective-permute-start.2 = (bf16[2,2,512,128]{3,2,1,0:T(8,128)(2,1)}, bf16[2,2,512,128]{3,2,1,0:T(8,128)(2,1)}, u32[]{:S(2)}, u32[]{:S(2)}) collective-permute-start(bf16[2,2,512,128]{3,2,1,0:T(8,128)(2,1)} %get-tuple-element.28.refs_0_), channel_id=1, source_target_pairs={{0,1},{1,0},{2,3},{3,2},{4,5},{5,4},{6,7},{7,6},{8,9},{9,8},{10,11... | collective-permute-start | bytes 1572872 | tf_op jit(solution)/shard_map/partner_2/ppermute | solution.py:285
  32.0 13.5 %collective-permute-done.6.refs_1_ = bf16[3,2,512,128]{3,2,1,0:T(8,128)(2,1)} collective-permute-done((bf16[3,2,512,128]{3,2,1,0:T(8,128)(2,1)S(1)}, bf16[3,2,512,128]{3,2,1,0:T(8,128)(2,1)}, u32[]{:S(2)}, u32[]{:S(2)}) %collective-permute-start.6) | collective-permute-done | bytes 786464 | tf_op jit(solution)/shard_map/partner_1/ppermute | solution.py:285
  45.5 1.9 %collective-permute-start.7 = (bf16[3,2,512,128]{3,2,1,0:T(8,128)(2,1)}, bf16[3,2,512,128]{3,2,1,0:T(8,128)(2,1)}, u32[]{:S(2)}, u32[]{:S(2)}) collective-permute-start(bf16[3,2,512,128]{3,2,1,0:T(8,128)(2,1)} %collective-permute-done.6.refs_1_), channel_id=1, source_target_pairs={{0,2},{2,4},{4,6},{6,8},{8,10},{10,12},{12,14},{14,16},{16,18},{18... | collective-permute-start | bytes 2359304 | tf_op jit(solution)/shard_map/onward_1/ppermute | solution.py:306
  47.4 1.6 %collective-permute-start.9 = (bf16[2,2,384,128]{3,2,1,0:T(8,128)(2,1)}, bf16[2,2,384,128]{3,2,1,0:T(8,128)(2,1)S(1)}, u32[]{:S(2)}, u32[]{:S(2)}) collective-permute-start(bf16[2,2,384,128]{3,2,1,0:T(8,128)(2,1)} %get-tuple-element.37), channel_id=1, source_target_pairs={{0,1},{1,0},{2,3},{3,2},{4,5},{5,4},{6,7},{7,6},{8,9},{9,8},{10,11... | collective-permute-start | bytes 1179656 | tf_op jit(solution)/shard_map/partner_3/ppermute | solution.py:285
  50.4 3.0 %attend_0.1.refs_3_ = bf16[512,512]{1,0:T(8,128)(2,1)S(1)} custom-call(s32[31]{0:T(128)S(1)} %concatenate.7.meta, bf16[4,512,128]{2,1,0:T(8,128)(2,1)S(1)} %copy-done.9, bf16[4,2,512,128]{3,2,1,0:T(8,128)(2,1)S(1)} %get-tuple-element.30.refs_0_, bf16[4,2,512,128]{3,2,1,0:T(8,128)(2,1)S(1)} %collective-permute-done.3.refs_1_, ...), custom_call_target="tpu_custom_call" | custom-call | tf_op jit(solution)/shard_map/attend_0/pallas_call | solution.py:219
  53.4 3.3 %collective-permute-done.2.refs_1_ = bf16[2,2,512,128]{3,2,1,0:T(8,128)(2,1)} collective-permute-done((bf16[2,2,512,128]{3,2,1,0:T(8,128)(2,1)}, bf16[2,2,512,128]{3,2,1,0:T(8,128)(2,1)}, u32[]{:S(2)}, u32[]{:S(2)}) %collective-permute-start.2) | collective-permute-done | bytes 524320 | tf_op jit(solution)/shard_map/partner_2/ppermute | solution.py:285
  56.7 1.9 %collective-permute-start.5 = (bf16[2,2,512,128]{3,2,1,0:T(8,128)(2,1)}, bf16[2,2,512,128]{3,2,1,0:T(8,128)(2,1)S(1)}, u32[]{:S(2)}, u32[]{:S(2)}) collective-permute-start(bf16[2,2,512,128]{3,2,1,0:T(8,128)(2,1)} %collective-permute-done.2.refs_1_), channel_id=1, source_target_pairs={{0,2},{2,4},{4,6},{6,8},{8,10},{10,12},{12,14},{14,16},{16,18},{18... | collective-permute-start | bytes 1572872 | tf_op jit(solution)/shard_map/onward_2/ppermute | solution.py:306
  58.6 1.6 %collective-permute-start = (bf16[1,2,384,128]{3,2,1,0:T(8,128)(2,1)}, bf16[1,2,384,128]{3,2,1,0:T(8,128)(2,1)S(1)}, u32[]{:S(2)}, u32[]{:S(2)}) collective-permute-start(bf16[1,2,384,128]{3,2,1,0:T(8,128)(2,1)} %copy-done.22), channel_id=1, source_target_pairs={{0,1},{1,0},{2,3},{3,2},{4,5},{5,4},{6,7},{7,6},{8,9},{9,8},{10,11... | collective-permute-start | bytes 589832 | tf_op jit(solution)/shard_map/partner_4/ppermute | solution.py:285
  62.3 3.4 %attend_1.1.refs_4_ = bf16[512,384]{1,0:T(8,128)(2,1)S(1)} custom-call(s32[31]{0:T(128)S(1)} %concatenate.7.meta, bf16[3,512,128]{2,1,0:T(8,128)(2,1)S(1)} %copy-done.11, bf16[3,2,512,128]{3,2,1,0:T(8,128)(2,1)S(1)} %copy-done.5, bf16[3,2,512,128]{3,2,1,0:T(8,128)(2,1)} %collective-permute-done.6.refs_1_, bf16[3,2,512,128]{3,2,1,0:T(8,128)(2,1)} %collective-permute-done.7.refs_2_), custom_call_target="tpu_custom_call" | custom-call | tf_op jit(solution)/shard_map/attend_1/pallas_call | solution.py:219
  65.7 2.1 %collective-permute-start.10 = (bf16[2,2,384,128]{3,2,1,0:T(8,128)(2,1)S(1)}, bf16[2,2,384,128]{3,2,1,0:T(8,128)(2,1)S(1)}, u32[]{:S(2)}, u32[]{:S(2)}) collective-permute-start(bf16[2,2,384,128]{3,2,1,0:T(8,128)(2,1)S(1)} %collective-permute-done.9.refs_1_), channel_id=1, source_target_pairs={{0,2},{2,4},{4,6},{6,8},{8,10},{10,12},{12,14},{14,16},{16,18},{18... | collective-permute-start | bytes 1179656 | tf_op jit(solution)/shard_map/onward_3/ppermute | solution.py:306
  67.9 2.7 %collective-permute-start.1 = (bf16[3,2,128,128]{3,2,1,0:T(8,128)(2,1)S(1)}, bf16[3,2,128,128]{3,2,1,0:T(8,128)(2,1)S(1)}, u32[]{:S(2)}, u32[]{:S(2)}) collective-permute-start(bf16[3,2,128,128]{3,2,1,0:T(8,128)(2,1)S(1)} %copy-done.21), channel_id=1, source_target_pairs={{0,1},{1,0},{2,3},{3,2},{4,5},{5,4},{6,7},{7,6},{8,9},{9,8},{10,11... | collective-permute-start | bytes 589832 | tf_op jit(solution)/shard_map/rest_5/ppermute | solution.py:285
  70.6 4.8 %attend_2.1.refs_6_ = f32[512,1536]{1,0:T(8,128)S(1)} custom-call(s32[31]{0:T(128)S(1)} %concatenate.7.meta, bf16[2,512,128]{2,1,0:T(8,128)(2,1)S(1)} %copy-done.17, bf16[2,2,512,128]{3,2,1,0:T(8,128)(2,1)} %get-tuple-element.28.refs_0_, bf16[2,2,512,128]{3,2,1,0:T(8,128)(2,1)} %collective-permute-done.2.refs_1_, ...), custom_call_target="tpu_custom_call" | custom-call | tf_op jit(solution)/shard_map/attend_2/pallas_call | solution.py:219
  75.4 2.2 %collective-permute-start.8 = (bf16[1,2,384,128]{3,2,1,0:T(8,128)(2,1)S(1)}, bf16[1,2,384,128]{3,2,1,0:T(8,128)(2,1)S(1)}, u32[]{:S(2)}, u32[]{:S(2)}) collective-permute-start(bf16[1,2,384,128]{3,2,1,0:T(8,128)(2,1)S(1)} %collective-permute-done.refs_1_), channel_id=1, source_target_pairs={{0,2},{2,4},{4,6},{6,8},{8,10},{10,12},{12,14},{14,16},{16,18},{18... | collective-permute-start | bytes 589832 | tf_op jit(solution)/shard_map/onward_4/ppermute | solution.py:306
  77.7 1.9 %attend_3.1.refs_4_ = bf16[512,256]{1,0:T(8,128)(2,1)S(1)} custom-call(s32[31]{0:T(128)S(1)} %concatenate.7.meta, bf16[2,512,128]{2,1,0:T(8,128)(2,1)S(1)} %copy-done.15, bf16[2,2,512,128]{3,2,1,0:T(8,128)(2,1)S(1)} %copy-done.7, bf16[2,2,384,128]{3,2,1,0:T(8,128)(2,1)S(1)} %collective-permute-done.9.refs_1_, ...), custom_call_target="tpu_custom_call" | custom-call | tf_op jit(solution)/shard_map/attend_3/pallas_call | solution.py:219
  79.7 3.8 %collective-permute-done.8.refs_3_ = bf16[1,2,384,128]{3,2,1,0:T(8,128)(2,1)S(1)} collective-permute-done((bf16[1,2,384,128]{3,2,1,0:T(8,128)(2,1)S(1)}, bf16[1,2,384,128]{3,2,1,0:T(8,128)(2,1)S(1)}, u32[]{:S(2)}, u32[]{:S(2)}) %collective-permute-start.8) | collective-permute-done | bytes 196640 | tf_op jit(solution)/shard_map/onward_4/ppermute | solution.py:306
  83.5 3.1 %attend_4.1 = bf16[512,1536]{1,0:T(8,128)(2,1)} custom-call(s32[31]{0:T(128)S(1)} %concatenate.7.meta, bf16[1,512,128]{2,1,0:T(8,128)(2,1)S(1)} %copy-done.19, bf16[1,2,512,128]{3,2,1,0:T(8,128)(2,1)S(1)} %copy-done.13, bf16[1,2,384,128]{3,2,1,0:T(8,128)(2,1)S(1)} %collective-permute-done.refs_1_, ...), custom_call_target="tpu_custom_call" | custom-call | tf_op jit(solution)/shard_map/attend_4/pallas_call | solution.py:219
  (62 shorter events, 11.5 us)
Async XLA Ops:
  2.2 26.3 %collective-permute-start.3 = (bf16[4,2,512,128]{3,2,1,0:T(8,128)(2,1)}, bf16[4,2,512,128]{3,2,1,0:T(8,128)(2,1)S(1)}, u32[]{:S(2)}, u32[]{:S(2)}) collective-permute-start(bf16[4,2,512,128]{3,2,1,0:T(8,128)(2,1)} %shard_map.64), channel_id=1, source_target_pairs={{0,1},{1,0},{2,3},{3,2},{4,5},{5,4},{6,7},{7,6},{8,9},{9,8},{10,11... | collective-permute-start | bytes 3145736 | tf_op jit(solution)/shard_map/partner_0/ppermute | solution.py:285
  3.8 1.4 %copy-start.1 = (bf16[512,1536]{1,0:T(8,128)(2,1)S(1)}, bf16[512,1536]{1,0:T(8,128)(2,1)}, u32[]{:S(2)}) copy-start(bf16[512,1536]{1,0:T(8,128)(2,1)} %refs_1_.3) | copy-start | bytes 4718596
  5.2 1.4 %copy-start.2 = (bf16[512,1536]{1,0:T(8,128)(2,1)S(1)}, bf16[512,1536]{1,0:T(8,128)(2,1)}, u32[]{:S(2)}) copy-start(bf16[512,1536]{1,0:T(8,128)(2,1)} %refs_2_.2) | copy-start | bytes 4718596
  6.6 1.4 %copy-start.3 = (bf16[512,1536]{1,0:T(8,128)(2,1)S(1)}, bf16[512,1536]{1,0:T(8,128)(2,1)}, u32[]{:S(2)}) copy-start(bf16[512,1536]{1,0:T(8,128)(2,1)} %refs_3_.1) | copy-start | bytes 4718596
  8.1 40.9 %copy-start.24 = (s32[8]{0:T(128)S(1)}, s32[8]{0:T(128)}, u32[]{:S(2)}) copy-start(s32[8]{0:T(128)} %param.10) | copy-start | bytes 100
  8.1 41.0 %copy-start.23 = (s32[8,5]{1,0:T(8,128)S(1)}, s32[8,5]{1,0:T(8,128)}, u32[]{:S(2)}) copy-start(s32[8,5]{1,0:T(8,128)} %param.9) | copy-start | bytes 484
  20.1 25.4 %collective-permute-start.6 = (bf16[3,2,512,128]{3,2,1,0:T(8,128)(2,1)S(1)}, bf16[3,2,512,128]{3,2,1,0:T(8,128)(2,1)}, u32[]{:S(2)}, u32[]{:S(2)}) collective-permute-start(bf16[3,2,512,128]{3,2,1,0:T(8,128)(2,1)S(1)} %get-tuple-element.33.refs_0_), channel_id=1, source_target_pairs={{0,1},{1,0},{2,3},{3,2},{4,5},{5,4},{6,7},{7,6},{8,9},{9,8},{10,11... | collective-permute-start | bytes 2359304 | tf_op jit(solution)/shard_map/partner_1/ppermute | solution.py:285
  28.5 20.8 %collective-permute-start.4 = (bf16[4,2,512,128]{3,2,1,0:T(8,128)(2,1)S(1)}, bf16[4,2,512,128]{3,2,1,0:T(8,128)(2,1)S(1)}, u32[]{:S(2)}, u32[]{:S(2)}) collective-permute-start(bf16[4,2,512,128]{3,2,1,0:T(8,128)(2,1)S(1)} %collective-permute-done.3.refs_1_), channel_id=1, source_target_pairs={{0,2},{2,4},{4,6},{6,8},{8,10},{10,12},{12,14},{14,16},{16,18},{18... | collective-permute-start | bytes 3145736 | tf_op jit(solution)/shard_map/onward_0/ppermute | solution.py:306
  30.4 26.3 %collective-permute-start.2 = (bf16[2,2,512,128]{3,2,1,0:T(8,128)(2,1)}, bf16[2,2,512,128]{3,2,1,0:T(8,128)(2,1)}, u32[]{:S(2)}, u32[]{:S(2)}) collective-permute-start(bf16[2,2,512,128]{3,2,1,0:T(8,128)(2,1)} %get-tuple-element.28.refs_0_), channel_id=1, source_target_pairs={{0,1},{1,0},{2,3},{3,2},{4,5},{5,4},{6,7},{7,6},{8,9},{9,8},{10,11... | collective-permute-start | bytes 1572872 | tf_op jit(solution)/shard_map/partner_2/ppermute | solution.py:285
  45.5 14.7 %collective-permute-start.7 = (bf16[3,2,512,128]{3,2,1,0:T(8,128)(2,1)}, bf16[3,2,512,128]{3,2,1,0:T(8,128)(2,1)}, u32[]{:S(2)}, u32[]{:S(2)}) collective-permute-start(bf16[3,2,512,128]{3,2,1,0:T(8,128)(2,1)} %collective-permute-done.6.refs_1_), channel_id=1, source_target_pairs={{0,2},{2,4},{4,6},{6,8},{8,10},{10,12},{12,14},{14,16},{16,18},{18... | collective-permute-start | bytes 2359304 | tf_op jit(solution)/shard_map/onward_1/ppermute | solution.py:306
  47.4 18.3 %collective-permute-start.9 = (bf16[2,2,384,128]{3,2,1,0:T(8,128)(2,1)}, bf16[2,2,384,128]{3,2,1,0:T(8,128)(2,1)S(1)}, u32[]{:S(2)}, u32[]{:S(2)}) collective-permute-start(bf16[2,2,384,128]{3,2,1,0:T(8,128)(2,1)} %get-tuple-element.37), channel_id=1, source_target_pairs={{0,1},{1,0},{2,3},{3,2},{4,5},{5,4},{6,7},{7,6},{8,9},{9,8},{10,11... | collective-permute-start | bytes 1179656 | tf_op jit(solution)/shard_map/partner_3/ppermute | solution.py:285
  50.4 20.2 %copy-start = (bf16[1536,1536]{1,0:T(8,128)(2,1)S(1)}, bf16[1536,1536]{1,0:T(8,128)(2,1)}, u32[]{:S(2)}) copy-start(bf16[1536,1536]{1,0:T(8,128)(2,1)} %refs_5_.3) | copy-start | bytes 14155780
  56.7 13.9 %collective-permute-start.5 = (bf16[2,2,512,128]{3,2,1,0:T(8,128)(2,1)}, bf16[2,2,512,128]{3,2,1,0:T(8,128)(2,1)S(1)}, u32[]{:S(2)}, u32[]{:S(2)}) collective-permute-start(bf16[2,2,512,128]{3,2,1,0:T(8,128)(2,1)} %collective-permute-done.2.refs_1_), channel_id=1, source_target_pairs={{0,2},{2,4},{4,6},{6,8},{8,10},{10,12},{12,14},{14,16},{16,18},{18... | collective-permute-start | bytes 1572872 | tf_op jit(solution)/shard_map/onward_2/ppermute | solution.py:306
  58.6 16.8 %collective-permute-start = (bf16[1,2,384,128]{3,2,1,0:T(8,128)(2,1)}, bf16[1,2,384,128]{3,2,1,0:T(8,128)(2,1)S(1)}, u32[]{:S(2)}, u32[]{:S(2)}) collective-permute-start(bf16[1,2,384,128]{3,2,1,0:T(8,128)(2,1)} %copy-done.22), channel_id=1, source_target_pairs={{0,1},{1,0},{2,3},{3,2},{4,5},{5,4},{6,7},{7,6},{8,9},{9,8},{10,11... | collective-permute-start | bytes 589832 | tf_op jit(solution)/shard_map/partner_4/ppermute | solution.py:285
  60.2 1.1 %copy-start.5 = (bf16[3,2,512,128]{3,2,1,0:T(8,128)(2,1)S(1)}, bf16[3,2,512,128]{3,2,1,0:T(8,128)(2,1)}, u32[]{:S(2)}) copy-start(bf16[3,2,512,128]{3,2,1,0:T(8,128)(2,1)} %copy-done.4) | copy-start | bytes 2359300
  62.3 5.5 %copy-start.21 = (bf16[3,2,128,128]{3,2,1,0:T(8,128)(2,1)S(1)}, bf16[3,2,128,128]{3,2,1,0:T(8,128)(2,1)}, u32[]{:S(2)}) copy-start(bf16[3,2,128,128]{3,2,1,0:T(8,128)(2,1)} %copy-done.20) | copy-start | bytes 589828
  62.3 8.3 %copy-start.17 = (bf16[2,512,128]{2,1,0:T(8,128)(2,1)S(1)}, bf16[2,512,128]{2,1,0:T(8,128)(2,1)}, u32[]{:S(2)}) copy-start(bf16[2,512,128]{2,1,0:T(8,128)(2,1)} %copy-done.16) | copy-start | bytes 786436
  65.7 12.0 %collective-permute-start.10 = (bf16[2,2,384,128]{3,2,1,0:T(8,128)(2,1)S(1)}, bf16[2,2,384,128]{3,2,1,0:T(8,128)(2,1)S(1)}, u32[]{:S(2)}, u32[]{:S(2)}) collective-permute-start(bf16[2,2,384,128]{3,2,1,0:T(8,128)(2,1)S(1)} %collective-permute-done.9.refs_1_), channel_id=1, source_target_pairs={{0,2},{2,4},{4,6},{6,8},{8,10},{10,12},{12,14},{14,16},{16,18},{18... | collective-permute-start | bytes 1179656 | tf_op jit(solution)/shard_map/onward_3/ppermute | solution.py:306
  67.9 9.8 %collective-permute-start.1 = (bf16[3,2,128,128]{3,2,1,0:T(8,128)(2,1)S(1)}, bf16[3,2,128,128]{3,2,1,0:T(8,128)(2,1)S(1)}, u32[]{:S(2)}, u32[]{:S(2)}) collective-permute-start(bf16[3,2,128,128]{3,2,1,0:T(8,128)(2,1)S(1)} %copy-done.21), channel_id=1, source_target_pairs={{0,1},{1,0},{2,3},{3,2},{4,5},{5,4},{6,7},{7,6},{8,9},{9,8},{10,11... | collective-permute-start | bytes 589832 | tf_op jit(solution)/shard_map/rest_5/ppermute | solution.py:285
  70.6 7.1 %copy-start.7 = (bf16[2,2,512,128]{3,2,1,0:T(8,128)(2,1)S(1)}, bf16[2,2,512,128]{3,2,1,0:T(8,128)(2,1)}, u32[]{:S(2)}) copy-start(bf16[2,2,512,128]{3,2,1,0:T(8,128)(2,1)} %copy-done.6) | copy-start | bytes 1572868
  70.6 7.1 %copy-start.15 = (bf16[2,512,128]{2,1,0:T(8,128)(2,1)S(1)}, bf16[2,512,128]{2,1,0:T(8,128)(2,1)}, u32[]{:S(2)}) copy-start(bf16[2,512,128]{2,1,0:T(8,128)(2,1)} %copy-done.14) | copy-start | bytes 786436
  75.4 8.1 %copy-start.13 = (bf16[1,2,512,128]{3,2,1,0:T(8,128)(2,1)S(1)}, bf16[1,2,512,128]{3,2,1,0:T(8,128)(2,1)}, u32[]{:S(2)}) copy-start(bf16[1,2,512,128]{3,2,1,0:T(8,128)(2,1)} %copy-done.12) | copy-start | bytes 786436
  75.4 8.0 %copy-start.19 = (bf16[1,512,128]{2,1,0:T(8,128)(2,1)S(1)}, bf16[1,512,128]{2,1,0:T(8,128)(2,1)}, u32[]{:S(2)}) copy-start(bf16[1,512,128]{2,1,0:T(8,128)(2,1)} %copy-done.18) | copy-start | bytes 393220
  75.4 8.0 %collective-permute-start.8 = (bf16[1,2,384,128]{3,2,1,0:T(8,128)(2,1)S(1)}, bf16[1,2,384,128]{3,2,1,0:T(8,128)(2,1)S(1)}, u32[]{:S(2)}, u32[]{:S(2)}) collective-permute-start(bf16[1,2,384,128]{3,2,1,0:T(8,128)(2,1)S(1)} %collective-permute-done.refs_1_), channel_id=1, source_target_pairs={{0,2},{2,4},{4,6},{6,8},{8,10},{10,12},{12,14},{14,16},{16,18},{18... | collective-permute-start | bytes 589832 | tf_op jit(solution)/shard_map/onward_4/ppermute | solution.py:306
  (12 other events, 9.4 us)

commit v2 on v0

--- a/solution.py
+++ b/solution.py
@@ -28,9 +28,27 @@
     return sizes + [heads - sum(sizes)]
 
 
+def cut_spots(tiles, rim):
+    member = lax.axis_index("ulysses")
+    return [member * (tiles - rim), (1 - member) * rim]
+
+
+def piece_spots(tiles, hops, rim, relay, parted):
+    if not relay:
+        return [tiles * hops] + [tiles * i for i in range(2 * hops + 1) if i != hops]
+    member = lax.axis_index("ulysses")
+    if not parted:
+        return [tiles, 2 * tiles * (1 - member), 2 * tiles * member]
+    return [
+        tiles,
+        (1 - member) * (3 * tiles - rim),
+        (1 - member) * 2 * tiles + member * rim,
+        (1 - member) * (tiles - rim) + member * 2 * tiles,
+    ]
+
+
 def pack_kernel(groups, q_groups, cuts, *refs):
     refs = list(refs)
-    cut_ref = refs.pop(0) if cuts else None
     q_ref, k_ref, v_ref = [refs.pop(0) for _ in range(3)]
     outs = [refs.pop(0) for _ in groups]
     q_outs = [refs.pop(0) for _ in q_groups]
@@ -74,9 +92,10 @@
     cut_jobs = []
     if cuts:
         size = groups[-1][1]
+        spots = cut_spots(rows // TILE, cuts[0])
         for h in range(size):
             for i, (extent, out) in enumerate(zip(cuts, cut_outs)):
-                part = pl.ds(pl.multiple_of(cut_ref[i] * TILE, TILE), extent * TILE)
+                part = pl.ds(pl.multiple_of(spots[i] * TILE, TILE), extent * TILE)
                 source = out_buf.at[len(jobs) - size + h, :, part]
                 cut_jobs.append(pltpu.make_async_copy(source, out.at[h], cut_sems.at[h, i]))
                 cut_jobs[-1].start()
@@ -91,7 +110,7 @@
         store.wait()
 
 
-def pack(cut_at, queries, keys, values, groups, q_groups, cuts, limit):
+def pack(queries, keys, values, groups, q_groups, cuts, limit):
     rows = keys.shape[0]
     heads = sum(size for _, size in groups)
     q_heads = sum(size for _, size in q_groups)
@@ -101,7 +120,7 @@
     return pl.pallas_call(
         functools.partial(pack_kernel, groups, q_groups, cuts),
         out_shape=[jax.ShapeDtypeStruct(shape, keys.dtype) for shape in shapes],
-        in_specs=[SMEM] * bool(cuts) + [HBM] * 3,
+        in_specs=[HBM] * 3,
         out_specs=[HBM] * len(shapes),
         scratch_shapes=[
             pltpu.VMEM((heads, rows, HD), keys.dtype),
@@ -113,11 +132,11 @@
         ],
         compiler_params=pltpu.CompilerParams(vmem_limit_bytes=limit),
         cost_estimate=pl.CostEstimate(flops=0, bytes_accessed=8 * rows * heads * HD, transcendentals=0),
-    )(*([cut_at] if cuts else []), queries, keys, values)
-
-
-def attend_kernel(cfg, meta, q_ref, *refs):
-    low, size, pieces, place_at, list_at, slots, spans, early, has_acc, final = cfg
+    )(queries, keys, values)
+
+
+def attend_kernel(cfg, tiles_ref, counts_ref, q_ref, *refs):
+    low, size, pieces, (hops, rim, relay, parted), early, has_acc, final = cfg
     refs = list(refs)
     piece_refs = [refs.pop(0) for _ in range(pieces)]
     early_refs = [refs.pop(0) for _ in early or ()]
@@ -126,6 +145,11 @@
     out_ref, kv_buf = refs[:2]
     rows = q_ref.shape[1]
     tiles = rows // TILE
+    slots = tiles_ref.shape[1]
+    spans = (2 * hops + 1) * rows
+    spots = piece_spots(tiles, hops, rim, relay, parted)
+    member, members = lax.axis_index("ulysses"), lax.axis_size("ulysses")
+    first = (lax.axis_index("temporal") * members + member - hops) * tiles
     att_buf, lead = out_ref, 0
     if early is not None:
         att_buf = refs[2]
@@ -137,9 +161,9 @@
     zeros = jnp.zeros((TILE, HD), jnp.bfloat16)
     places, v_places, ones = [], [], []
     for tile in range(tiles):
-        row = list_at + tile * (slots + 1)
-        live = meta[row]
-        at = [pl.multiple_of(meta[row + 1 + j] * TILE, TILE) for j in range(slots)]
+        row = member * tiles + tile
+        live = counts_ref[row]
+        at = [pl.multiple_of((tiles_ref[row, j] - first) * TILE, TILE) for j in range(slots)]
         places.append(at)
         v_places.append([pl.multiple_of(jnp.where(j < live, at[j], spans), TILE) for j in range(slots)])
         ones.append([zeros + jnp.where(j < live, 1.0, 0.0).astype(jnp.bfloat16) for j in range(slots)])
@@ -165,7 +189,7 @@
 
     def ready(h):
         for i, ref in enumerate(piece_refs):
-            place = pl.ds(pl.multiple_of(meta[place_at + i] * TILE, TILE), ref.shape[2])
+            place = pl.ds(pl.multiple_of(spots[i] * TILE, TILE), ref.shape[2])
             for part in range(2):
                 kv_buf[h % 2, part, place] = ref[h, part]
         kv_buf[h % 2, 1, spans : spans + TILE] = zeros
@@ -200,13 +224,13 @@
         copy.wait()
 
 
-def attend(meta, layout, queries, pieces, span, early, out_weight, acc, final):
+def attend(tile_list, counts, layout, queries, pieces, span, early, out_weight, acc, final):
     rows = queries.shape[1]
     low, size = span
-    place_at, list_at, slots, reach = layout
+    reach = (2 * layout[0] + 1) * rows
     width = out_weight.shape[1]
     bf16 = jnp.bfloat16
-    operands = [meta, queries, *pieces]
+    operands = [tile_list, counts, queries, *pieces]
     scratch = [pltpu.VMEM((2, 2, reach + TILE, HD), bf16)]
     parts = None
     out_shape = jax.ShapeDtypeStruct((rows, size * HD), bf16)
@@ -221,10 +245,10 @@
             scratch += [pltpu.VMEM((rows, width), bf16), pltpu.SemaphoreType.DMA((-(-width // STRIP),))]
     return pl.pallas_call(
         functools.partial(
-            attend_kernel, (low, size, len(pieces), place_at, list_at, slots, reach, parts, acc is not None, final)
+            attend_kernel, (low, size, len(pieces), layout, parts, acc is not None, final)
         ),
         out_shape=out_shape,
-        in_specs=[SMEM] + [VMEM] * (len(operands) - 1),
+        in_specs=[SMEM] * 2 + [VMEM] * (len(operands) - 2),
         out_specs=HBM if final else VMEM,
         scratch_shapes=scratch,
         compiler_params=pltpu.CompilerParams(vmem_limit_bytes=VMEM_LIMIT),
@@ -240,38 +264,20 @@
     rows, model = queries.shape
     tiles = rows // TILE
     groups, members = lax.axis_size("temporal"), lax.axis_size("ulysses")
-    group, member = lax.axis_index("temporal"), lax.axis_index("ulysses")
     total = groups * members
     both = ("temporal", "ulysses")
     hops = -(-REACH // tiles)
     relay = members == 2 and hops == 1
     rim = min(REACH, tiles)
     cuts = [rim, tiles - rim] if relay and tiles > rim else []
-    whole_at = [tiles * hops] + [tiles * i for i in range(2 * hops + 1) if i != hops]
-    cut_at = [member * (tiles - rim), (1 - member) * rim]
-    part_at = []
-    if relay:
-        whole_at = [tiles, 2 * tiles * (1 - member), 2 * tiles * member]
-        part_at = [
-            tiles,
-            (1 - member) * (3 * tiles - rim),
-            (1 - member) * 2 * tiles + member * rim,
-            (1 - member) * (tiles - rim) + member * 2 * tiles,
-        ]
-    first = ((group * members + member) - hops) * tiles
-    slots = tile_list.shape[1]
-    lists = jnp.concatenate([counts[:, None], tile_list - first], axis=1)
-    lists = lax.dynamic_slice_in_dim(lists, member * tiles, tiles, axis=0)
-    meta = jnp.concatenate([jnp.stack([jnp.asarray(x, jnp.int32) for x in whole_at + part_at]), lists.reshape(-1)])
-    cut_at = jnp.stack([jnp.asarray(x, jnp.int32) for x in cut_at])
 
     spans, low = [], 0
     for size in split_heads(model // HD):
         spans.append((low, size))
         low += size
     count = len(spans)
-    sent = pack(None, queries, keys, values, spans[:1], [], [], VMEM_WHOLE)
-    laid = pack(cut_at, queries, after(keys, *sent), values, spans, spans, cuts, VMEM_LIMIT)
+    sent = pack(queries, keys, values, spans[:1], [], [], VMEM_WHOLE)
+    laid = pack(queries, after(keys, *sent), values, spans, spans, cuts, VMEM_LIMIT)
     blocks, heads_of, parts = laid[:count], laid[count : 2 * count], laid[2 * count :]
     sent = [[block] for block in (*sent, *blocks[1:])]
     if parts and count > 1:
@@ -312,10 +318,9 @@
                 early = results[max(mid + 1, 0) :]
             elif j == mid:
                 early = results[:]
-            split = relay and len(sent[j]) > 1
-            layout = (len(whole_at) if split else 0, meta.shape[0] - lists.size, slots, len(whole_at) * rows)
+            layout = (hops, rim, relay, len(sent[j]) > 1)
             with jax.named_scope(f"attend_{j}"):
-                result = attend(meta, layout, heads_of[j], held, spans[j], early, out_weight, acc if final else None, final)
+                result = attend(tile_list, counts, layout, heads_of[j], held, spans[j], early, out_weight, acc if final else None, final)
             results.append(result)
             if j == mid:
                 acc = result

time: 84 us -> 83.6 us (level)
  waiting for transfers between devices: 29.2 us -> 38.6 us
  local copies, waits for them, and re-layouts: 10.6 us -> 4.24 us
  Pallas kernels: 24.7 us -> 21.7 us
    ppermute x6, waiting for transfers between devices: 28.1 us -> 36.1 us  [on_device(): near[-1].append(lax.ppermute(block, 'ulysses', swap))]
    unnamed x38 -> x14, local copies, waits for them, and re-layouts: 10.4 us -> 4.24 us
    pallas_call x5, Pallas kernels: 17 us -> 14.5 us  [attend(): pl.pallas_call(functools.partial(attend_kernel, (low, size, len(pieces),...]
    ppermute x5, waiting for transfers between devices: 1.14 us -> 2.51 us  [on_device(): pieces.append(lax.ppermute(gate, both, onward))]
  transfers between devices with their start and end apart: 11 -> 11, of which waited for: 7 -> 8; matrix products, arithmetic and copies ran while one was open for 0% -> 0% of each run, Pallas kernels for 23% -> 19%
where the time goes in v2:
time: 83.6 us; the launch traced here: 83.3 us
  waiting for transfers between devices  38.6 us (46%)
  Pallas kernels  21.7 us (26%)
  starting transfers between devices  18.4 us (22%)
  local copies, waits for them, and re-layouts  4.24 us (5%)
    ppermute x6, waiting for transfers between devices, on_device(): near[-1].append(lax.ppermute(block, 'ulysses', swap))  36.1 us
    pallas_call x5, Pallas kernels, attend(): pl.pallas_call(functools.partial(attend_kernel, (low, size, len(pieces),...  14.5 us
    ppermute x5, starting transfers between devices, on_device(): pieces.append(lax.ppermute(gate, both, onward))  9.73 us
    ppermute x6, starting transfers between devices, on_device(): near[-1].append(lax.ppermute(block, 'ulysses', swap))  8.68 us
    pallas_call x2, Pallas kernels, pack(): pl.pallas_call(functools.partial(pack_kernel, groups, q_groups, cuts), ou...  7.28 us
    unnamed x14, local copies, waits for them, and re-layouts  4.24 us
    ppermute x5, waiting for transfers between devices, on_device(): pieces.append(lax.ppermute(gate, both, onward))  2.51 us
  transfers between devices with their start and end apart: 11, of which 8 were waited for; matrix products, arithmetic and copies ran while one was open for 0% of the time, Pallas kernels for 19%

profile of v2, /device:TPU:8, one launch (start us, length us, event | category | flops | bytes accessed | tf_op | source)
XLA Modules:
  0.0 83.3 jit_solution(10559607476355054173)
XLA Ops:
  0.0 2.1 %shard_map.64 = bf16[3,2,512,128]{3,2,1,0:T(8,128)(2,1)} custom-call(bf16[512,1536]{1,0:T(8,128)(2,1)} %refs_0_.3, bf16[512,1536]{1,0:T(8,128)(2,1)} %refs_1_.2, bf16[512,1536]{1,0:T(8,128)(2,1)} %refs_2_.3), custom_call_target="tpu_custom_call" | custom-call | bytes 1572864 | tf_op jit(solution)/shard_map/pallas_call | solution.py:120
  2.2 1.6 %collective-permute-start.3 = (bf16[3,2,512,128]{3,2,1,0:T(8,128)(2,1)}, bf16[3,2,512,128]{3,2,1,0:T(8,128)(2,1)S(1)}, u32[]{:S(2)}, u32[]{:S(2)}) collective-permute-start(bf16[3,2,512,128]{3,2,1,0:T(8,128)(2,1)} %shard_map.64), channel_id=1, source_target_pairs={{0,1},{1,0},{2,3},{3,2},{4,5},{5,4},{6,7},{7,6},{8,9},{9,8},{10,11... | collective-permute-start | bytes 2359304 | tf_op jit(solution)/shard_map/partner_0/ppermute | solution.py:295
  8.0 5.1 %shard_map.65 = (bf16[3,2,512,128]{3,2,1,0:T(8,128)(2,1)S(1)}, bf16[3,2,512,128]{3,2,1,0:T(8,128)(2,1)S(1)}, bf16[2,2,512,128]{3,2,1,0:T(8,128)(2,1)S(1)}, bf16[...) custom-call(bf16[512,1536]{1,0:T(8,128)(2,1)S(1)} %copy-done, ...), custom_call_target="tpu_custom_call" | custom-call | bytes 6291456 | tf_op jit(solution)/shard_map/pallas_call | solution.py:120
  14.0 8.9 %collective-permute-done.3.refs_1_ = bf16[3,2,512,128]{3,2,1,0:T(8,128)(2,1)S(1)} collective-permute-done((bf16[3,2,512,128]{3,2,1,0:T(8,128)(2,1)}, bf16[3,2,512,128]{3,2,1,0:T(8,128)(2,1)S(1)}, u32[]{:S(2)}, u32[]{:S(2)}) %collective-permute-start.3) | collective-permute-done | bytes 786464 | tf_op jit(solution)/shard_map/partner_0/ppermute | solution.py:295
  22.9 1.9 %collective-permute-start.4 = (bf16[3,2,512,128]{3,2,1,0:T(8,128)(2,1)S(1)}, bf16[3,2,512,128]{3,2,1,0:T(8,128)(2,1)S(1)}, u32[]{:S(2)}, u32[]{:S(2)}) collective-permute-start(bf16[3,2,512,128]{3,2,1,0:T(8,128)(2,1)S(1)} %collective-permute-done.3.refs_1_), channel_id=1, source_target_pairs={{0,2},{2,4},{4,6},{6,8},{8,10},{10,12},{12,14},{14,16},{16,18},{18... | collective-permute-start | bytes 2359304 | tf_op jit(solution)/shard_map/onward_0/ppermute | solution.py:312
  24.8 1.6 %collective-permute-start.2 = (bf16[2,2,512,128]{3,2,1,0:T(8,128)(2,1)S(1)}, bf16[2,2,512,128]{3,2,1,0:T(8,128)(2,1)S(1)}, u32[]{:S(2)}, u32[]{:S(2)}) collective-permute-start(bf16[2,2,512,128]{3,2,1,0:T(8,128)(2,1)S(1)} %get-tuple-element.27.refs_0_), channel_id=1, source_target_pairs={{0,1},{1,0},{2,3},{3,2},{4,5},{5,4},{6,7},{7,6},{8,9},{9,8},{10,11... | collective-permute-start | bytes 1572872 | tf_op jit(solution)/shard_map/partner_2/ppermute | solution.py:295
  26.3 13.4 %collective-permute-done.6.refs_1_ = bf16[3,2,512,128]{3,2,1,0:T(8,128)(2,1)S(1)} collective-permute-done((bf16[3,2,512,128]{3,2,1,0:T(8,128)(2,1)S(1)}, bf16[3,2,512,128]{3,2,1,0:T(8,128)(2,1)S(1)}, u32[]{:S(2)}, u32[]{:S(2)}) %collective-permute-start.6) | collective-permute-done | bytes 786464 | tf_op jit(solution)/shard_map/partner_1/ppermute | solution.py:295
  39.7 1.9 %collective-permute-start.7 = (bf16[3,2,512,128]{3,2,1,0:T(8,128)(2,1)S(1)}, bf16[3,2,512,128]{3,2,1,0:T(8,128)(2,1)S(1)}, u32[]{:S(2)}, u32[]{:S(2)}) collective-permute-start(bf16[3,2,512,128]{3,2,1,0:T(8,128)(2,1)S(1)} %collective-permute-done.6.refs_1_), channel_id=1, source_target_pairs={{0,2},{2,4},{4,6},{6,8},{8,10},{10,12},{12,14},{14,16},{16,18},{18... | collective-permute-start | bytes 2359304 | tf_op jit(solution)/shard_map/onward_1/ppermute | solution.py:312
  41.6 1.6 %collective-permute-start.9 = (bf16[2,2,512,128]{3,2,1,0:T(8,128)(2,1)S(1)}, bf16[2,2,512,128]{3,2,1,0:T(8,128)(2,1)S(1)}, u32[]{:S(2)}, u32[]{:S(2)}) collective-permute-start(bf16[2,2,512,128]{3,2,1,0:T(8,128)(2,1)S(1)} %get-tuple-element.35.refs_0_), channel_id=1, source_target_pairs={{0,1},{1,0},{2,3},{3,2},{4,5},{5,4},{6,7},{7,6},{8,9},{9,8},{10,11... | collective-permute-start | bytes 1572872 | tf_op jit(solution)/shard_map/partner_3/ppermute | solution.py:295
  43.2 2.6 %attend_0.1.refs_3_ = bf16[512,384]{1,0:T(8,128)(2,1)S(1)} custom-call(s32[8,5]{1,0:T(8,128)S(1)} %copy-done.3, s32[8]{0:T(128)S(1)} %copy-done.4, bf16[3,512,128]{2,1,0:T(8,128)(2,1)S(1)} %get-tuple-element.28.q_ref, bf16[3,2,512,128]{3,2,1,0:T(8,128)(2,1)S(1)} %get-tuple-element.29.refs_0_, bf16[3,2,512,128]{3,2,1,0:T(8,128)(2,1)S(1)} %collective-permute-done.3.refs_1_, ...), custom_call_target="tpu_custom_call" | custom-call | tf_op jit(solution)/shard_map/attend_0/pallas_call | solution.py:246
  45.8 5.2 %collective-permute-done.2.refs_1_ = bf16[2,2,512,128]{3,2,1,0:T(8,128)(2,1)S(1)} collective-permute-done((bf16[2,2,512,128]{3,2,1,0:T(8,128)(2,1)S(1)}, bf16[2,2,512,128]{3,2,1,0:T(8,128)(2,1)S(1)}, u32[]{:S(2)}, u32[]{:S(2)}) %collective-permute-start.2) | collective-permute-done | bytes 524320 | tf_op jit(solution)/shard_map/partner_2/ppermute | solution.py:295
  51.0 1.9 %collective-permute-start.5 = (bf16[2,2,512,128]{3,2,1,0:T(8,128)(2,1)S(1)}, bf16[2,2,512,128]{3,2,1,0:T(8,128)(2,1)S(1)}, u32[]{:S(2)}, u32[]{:S(2)}) collective-permute-start(bf16[2,2,512,128]{3,2,1,0:T(8,128)(2,1)S(1)} %collective-permute-done.2.refs_1_), channel_id=1, source_target_pairs={{0,2},{2,4},{4,6},{6,8},{8,10},{10,12},{12,14},{14,16},{16,18},{18... | collective-permute-start | bytes 1572872 | tf_op jit(solution)/shard_map/onward_2/ppermute | solution.py:312
  52.9 1.6 %collective-permute-start = (bf16[2,2,384,128]{3,2,1,0:T(8,128)(2,1)S(1)}, bf16[2,2,384,128]{3,2,1,0:T(8,128)(2,1)S(1)}, u32[]{:S(2)}, u32[]{:S(2)}) collective-permute-start(bf16[2,2,384,128]{3,2,1,0:T(8,128)(2,1)S(1)} %get-tuple-element.24), channel_id=1, source_target_pairs={{0,1},{1,0},{2,3},{3,2},{4,5},{5,4},{6,7},{7,6},{8,9},{9,8},{10,11... | collective-permute-start | bytes 1179656 | tf_op jit(solution)/shard_map/partner_4/ppermute | solution.py:295
  54.4 2.6 %attend_1.1.refs_4_ = bf16[512,384]{1,0:T(8,128)(2,1)S(1)} custom-call(s32[8,5]{1,0:T(8,128)S(1)} %copy-done.3, s32[8]{0:T(128)S(1)} %copy-done.4, bf16[3,512,128]{2,1,0:T(8,128)(2,1)S(1)} %get-tuple-element.31.q_ref, bf16[3,2,512,128]{3,2,1,0:T(8,128)(2,1)S(1)} %get-tuple-element.32.refs_0_, bf16[3,2,512,128]{3,2,1,0:T(8,128)(2,1)S(1)} %collective-permute-done.6.refs_1_, ...), custom_call_target="tpu_custom_call" | custom-call | tf_op jit(solution)/shard_map/attend_1/pallas_call | solution.py:246
  57.0 5.2 %collective-permute-done.9.refs_1_ = bf16[2,2,512,128]{3,2,1,0:T(8,128)(2,1)S(1)} collective-permute-done((bf16[2,2,512,128]{3,2,1,0:T(8,128)(2,1)S(1)}, bf16[2,2,512,128]{3,2,1,0:T(8,128)(2,1)S(1)}, u32[]{:S(2)}, u32[]{:S(2)}) %collective-permute-start.9) | collective-permute-done | bytes 524320 | tf_op jit(solution)/shard_map/partner_3/ppermute | solution.py:295
  62.2 1.9 %collective-permute-start.10 = (bf16[2,2,512,128]{3,2,1,0:T(8,128)(2,1)S(1)}, bf16[2,2,512,128]{3,2,1,0:T(8,128)(2,1)S(1)}, u32[]{:S(2)}, u32[]{:S(2)}) collective-permute-start(bf16[2,2,512,128]{3,2,1,0:T(8,128)(2,1)S(1)} %collective-permute-done.9.refs_1_), channel_id=1, source_target_pairs={{0,2},{2,4},{4,6},{6,8},{8,10},{10,12},{12,14},{14,16},{16,18},{18... | collective-permute-start | bytes 1572872 | tf_op jit(solution)/shard_map/onward_3/ppermute | solution.py:312
  64.2 3.6 %attend_2.1.refs_6_ = f32[512,1536]{1,0:T(8,128)S(1)} custom-call(s32[8,5]{1,0:T(8,128)S(1)} %copy-done.3, s32[8]{0:T(128)S(1)} %copy-done.4, bf16[2,512,128]{2,1,0:T(8,128)(2,1)S(1)} %get-tuple-element.26.q_ref, bf16[2,2,512,128]{3,2,1,0:T(8,128)(2,1)S(1)} %get-tuple-element.27.refs_0_, bf16[2,2,512,128]{3,2,1,0:T(8,128)(2,1)S(1)} %collective-permute-done.2.refs_1_, ...), custom_call_target="tpu_custom_call" | custom-call | tf_op jit(solution)/shard_map/attend_2/pallas_call | solution.py:246
  67.8 1.7 %collective-permute-done.refs_1_ = bf16[2,2,384,128]{3,2,1,0:T(8,128)(2,1)S(1)} collective-permute-done((bf16[2,2,384,128]{3,2,1,0:T(8,128)(2,1)S(1)}, bf16[2,2,384,128]{3,2,1,0:T(8,128)(2,1)S(1)}, u32[]{:S(2)}, u32[]{:S(2)}) %collective-permute-start) | collective-permute-done | bytes 393248 | tf_op jit(solution)/shard_map/partner_4/ppermute | solution.py:295
  69.5 2.1 %collective-permute-start.8 = (bf16[2,2,384,128]{3,2,1,0:T(8,128)(2,1)S(1)}, bf16[2,2,384,128]{3,2,1,0:T(8,128)(2,1)S(1)}, u32[]{:S(2)}, u32[]{:S(2)}) collective-permute-start(bf16[2,2,384,128]{3,2,1,0:T(8,128)(2,1)S(1)} %collective-permute-done.refs_1_), channel_id=1, source_target_pairs={{0,2},{2,4},{4,6},{6,8},{8,10},{10,12},{12,14},{14,16},{16,18},{18... | collective-permute-start | bytes 1179656 | tf_op jit(solution)/shard_map/onward_4/ppermute | solution.py:312
  71.6 1.6 %collective-permute-start.1 = (bf16[2,2,128,128]{3,2,1,0:T(8,128)(2,1)S(1)}, bf16[2,2,128,128]{3,2,1,0:T(8,128)(2,1)S(1)}, u32[]{:S(2)}, u32[]{:S(2)}) collective-permute-start(bf16[2,2,128,128]{3,2,1,0:T(8,128)(2,1)S(1)} %get-tuple-element.25), channel_id=1, source_target_pairs={{0,1},{1,0},{2,3},{3,2},{4,5},{5,4},{6,7},{7,6},{8,9},{9,8},{10,11... | collective-permute-start | bytes 393224 | tf_op jit(solution)/shard_map/rest_4/ppermute | solution.py:295
  73.6 2.0 %attend_3.1.refs_4_ = bf16[512,256]{1,0:T(8,128)(2,1)S(1)} custom-call(s32[8,5]{1,0:T(8,128)S(1)} %copy-done.3, s32[8]{0:T(128)S(1)} %copy-done.4, bf16[2,512,128]{2,1,0:T(8,128)(2,1)S(1)} %get-tuple-element.34.q_ref, bf16[2,2,512,128]{3,2,1,0:T(8,128)(2,1)S(1)} %get-tuple-element.35.refs_0_, bf16[2,2,512,128]{3,2,1,0:T(8,128)(2,1)S(1)} %collective-permute-done.9.refs_1_, ...), custom_call_target="tpu_custom_call" | custom-call | tf_op jit(solution)/shard_map/attend_3/pallas_call | solution.py:246
  75.6 1.8 %collective-permute-done.1.refs_2_ = bf16[2,2,128,128]{3,2,1,0:T(8,128)(2,1)S(1)} collective-permute-done((bf16[2,2,128,128]{3,2,1,0:T(8,128)(2,1)S(1)}, bf16[2,2,128,128]{3,2,1,0:T(8,128)(2,1)S(1)}, u32[]{:S(2)}, u32[]{:S(2)}) %collective-permute-start.1) | collective-permute-done | bytes 131104 | tf_op jit(solution)/shard_map/rest_4/ppermute | solution.py:295
  77.4 2.1 %collective-permute-done.8.refs_3_ = bf16[2,2,384,128]{3,2,1,0:T(8,128)(2,1)S(1)} collective-permute-done((bf16[2,2,384,128]{3,2,1,0:T(8,128)(2,1)S(1)}, bf16[2,2,384,128]{3,2,1,0:T(8,128)(2,1)S(1)}, u32[]{:S(2)}, u32[]{:S(2)}) %collective-permute-start.8) | collective-permute-done | bytes 393248 | tf_op jit(solution)/shard_map/onward_4/ppermute | solution.py:312
  79.5 3.7 %attend_4.1 = bf16[512,1536]{1,0:T(8,128)(2,1)} custom-call(s32[8,5]{1,0:T(8,128)S(1)} %copy-done.3, s32[8]{0:T(128)S(1)} %copy-done.4, bf16[2,512,128]{2,1,0:T(8,128)(2,1)S(1)} %get-tuple-element.22.q_ref, bf16[2,2,512,128]{3,2,1,0:T(8,128)(2,1)S(1)} %get-tuple-element.23.refs_0_, bf16[2,2,384,128]{3,2,1,0:T(8,128)(2,1)S(1)} %collective-permute-done.refs_1_, ...), custom_call_target="tpu_custom_call" | custom-call | tf_op jit(solution)/shard_map/attend_4/pallas_call | solution.py:246
  (20 shorter events, 5.6 us)
Async XLA Ops:
  0.0 64.1 %slice-start = ((s8[4718592]{0:T(1024)(128)(4,1)}), s8[524288]{0:T(1024)(128)(4,1)S(1)}, s32[]{:S(2)}) async-start(s8[4718592]{0:T(1024)(128)(4,1)} %bitcast), calls=%async_computation | async-start | bytes 1048576
  2.2 62.0 %slice-start.1 = ((s8[4718592]{0:T(1024)(128)(4,1)}), s8[4194304]{0:T(1024)(128)(4,1)S(1)}, s32[]{:S(2)}) async-start(s8[4718592]{0:T(1024)(128)(4,1)} %bitcast), calls=%async_computation.1 | async-start | bytes 8388608
  2.2 20.7 %collective-permute-start.3 = (bf16[3,2,512,128]{3,2,1,0:T(8,128)(2,1)}, bf16[3,2,512,128]{3,2,1,0:T(8,128)(2,1)S(1)}, u32[]{:S(2)}, u32[]{:S(2)}) collective-permute-start(bf16[3,2,512,128]{3,2,1,0:T(8,128)(2,1)} %shard_map.64), channel_id=1, source_target_pairs={{0,1},{1,0},{2,3},{3,2},{4,5},{5,4},{6,7},{7,6},{8,9},{9,8},{10,11... | collective-permute-start | bytes 2359304 | tf_op jit(solution)/shard_map/partner_0/ppermute | solution.py:295
  3.7 1.4 %copy-start = (bf16[512,1536]{1,0:T(8,128)(2,1)S(1)}, bf16[512,1536]{1,0:T(8,128)(2,1)}, u32[]{:S(2)}) copy-start(bf16[512,1536]{1,0:T(8,128)(2,1)} %refs_0_.3) | copy-start | bytes 4718596
  5.1 1.4 %copy-start.1 = (bf16[512,1536]{1,0:T(8,128)(2,1)S(1)}, bf16[512,1536]{1,0:T(8,128)(2,1)}, u32[]{:S(2)}) copy-start(bf16[512,1536]{1,0:T(8,128)(2,1)} %refs_1_.2) | copy-start | bytes 4718596
  6.5 1.4 %copy-start.2 = (bf16[512,1536]{1,0:T(8,128)(2,1)S(1)}, bf16[512,1536]{1,0:T(8,128)(2,1)}, u32[]{:S(2)}) copy-start(bf16[512,1536]{1,0:T(8,128)(2,1)} %refs_2_.3) | copy-start | bytes 4718596
  7.9 35.3 %copy-start.3 = (s32[8,5]{1,0:T(8,128)S(1)}, s32[8,5]{1,0:T(8,128)}, u32[]{:S(2)}) copy-start(s32[8,5]{1,0:T(8,128)} %tiles_ref.9) | copy-start | bytes 484
  8.0 35.3 %copy-start.4 = (s32[8]{0:T(128)S(1)}, s32[8]{0:T(128)}, u32[]{:S(2)}) copy-start(s32[8]{0:T(128)} %counts_ref.9) | copy-start | bytes 100
  13.1 26.6 %collective-permute-start.6 = (bf16[3,2,512,128]{3,2,1,0:T(8,128)(2,1)S(1)}, bf16[3,2,512,128]{3,2,1,0:T(8,128)(2,1)S(1)}, u32[]{:S(2)}, u32[]{:S(2)}) collective-permute-start(bf16[3,2,512,128]{3,2,1,0:T(8,128)(2,1)S(1)} %get-tuple-element.32.refs_0_), channel_id=1, source_target_pairs={{0,1},{1,0},{2,3},{3,2},{4,5},{5,4},{6,7},{7,6},{8,9},{9,8},{10,11... | collective-permute-start | bytes 2359304 | tf_op jit(solution)/shard_map/partner_1/ppermute | solution.py:295
  22.9 20.3 %collective-permute-start.4 = (bf16[3,2,512,128]{3,2,1,0:T(8,128)(2,1)S(1)}, bf16[3,2,512,128]{3,2,1,0:T(8,128)(2,1)S(1)}, u32[]{:S(2)}, u32[]{:S(2)}) collective-permute-start(bf16[3,2,512,128]{3,2,1,0:T(8,128)(2,1)S(1)} %collective-permute-done.3.refs_1_), channel_id=1, source_target_pairs={{0,2},{2,4},{4,6},{6,8},{8,10},{10,12},{12,14},{14,16},{16,18},{18... | collective-permute-start | bytes 2359304 | tf_op jit(solution)/shard_map/onward_0/ppermute | solution.py:312
  24.8 26.2 %collective-permute-start.2 = (bf16[2,2,512,128]{3,2,1,0:T(8,128)(2,1)S(1)}, bf16[2,2,512,128]{3,2,1,0:T(8,128)(2,1)S(1)}, u32[]{:S(2)}, u32[]{:S(2)}) collective-permute-start(bf16[2,2,512,128]{3,2,1,0:T(8,128)(2,1)S(1)} %get-tuple-element.27.refs_0_), channel_id=1, source_target_pairs={{0,1},{1,0},{2,3},{3,2},{4,5},{5,4},{6,7},{7,6},{8,9},{9,8},{10,11... | collective-permute-start | bytes 1572872 | tf_op jit(solution)/shard_map/partner_2/ppermute | solution.py:295
  39.7 14.7 %collective-permute-start.7 = (bf16[3,2,512,128]{3,2,1,0:T(8,128)(2,1)S(1)}, bf16[3,2,512,128]{3,2,1,0:T(8,128)(2,1)S(1)}, u32[]{:S(2)}, u32[]{:S(2)}) collective-permute-start(bf16[3,2,512,128]{3,2,1,0:T(8,128)(2,1)S(1)} %collective-permute-done.6.refs_1_), channel_id=1, source_target_pairs={{0,2},{2,4},{4,6},{6,8},{8,10},{10,12},{12,14},{14,16},{16,18},{18... | collective-permute-start | bytes 2359304 | tf_op jit(solution)/shard_map/onward_1/ppermute | solution.py:312
  41.6 20.6 %collective-permute-start.9 = (bf16[2,2,512,128]{3,2,1,0:T(8,128)(2,1)S(1)}, bf16[2,2,512,128]{3,2,1,0:T(8,128)(2,1)S(1)}, u32[]{:S(2)}, u32[]{:S(2)}) collective-permute-start(bf16[2,2,512,128]{3,2,1,0:T(8,128)(2,1)S(1)} %get-tuple-element.35.refs_0_), channel_id=1, source_target_pairs={{0,1},{1,0},{2,3},{3,2},{4,5},{5,4},{6,7},{7,6},{8,9},{9,8},{10,11... | collective-permute-start | bytes 1572872 | tf_op jit(solution)/shard_map/partner_3/ppermute | solution.py:295
  51.0 13.2 %collective-permute-start.5 = (bf16[2,2,512,128]{3,2,1,0:T(8,128)(2,1)S(1)}, bf16[2,2,512,128]{3,2,1,0:T(8,128)(2,1)S(1)}, u32[]{:S(2)}, u32[]{:S(2)}) collective-permute-start(bf16[2,2,512,128]{3,2,1,0:T(8,128)(2,1)S(1)} %collective-permute-done.2.refs_1_), channel_id=1, source_target_pairs={{0,2},{2,4},{4,6},{6,8},{8,10},{10,12},{12,14},{14,16},{16,18},{18... | collective-permute-start | bytes 1572872 | tf_op jit(solution)/shard_map/onward_2/ppermute | solution.py:312
  52.9 16.6 %collective-permute-start = (bf16[2,2,384,128]{3,2,1,0:T(8,128)(2,1)S(1)}, bf16[2,2,384,128]{3,2,1,0:T(8,128)(2,1)S(1)}, u32[]{:S(2)}, u32[]{:S(2)}) collective-permute-start(bf16[2,2,384,128]{3,2,1,0:T(8,128)(2,1)S(1)} %get-tuple-element.24), channel_id=1, source_target_pairs={{0,1},{1,0},{2,3},{3,2},{4,5},{5,4},{6,7},{7,6},{8,9},{9,8},{10,11... | collective-permute-start | bytes 1179656 | tf_op jit(solution)/shard_map/partner_4/ppermute | solution.py:295
  62.2 11.4 %collective-permute-start.10 = (bf16[2,2,512,128]{3,2,1,0:T(8,128)(2,1)S(1)}, bf16[2,2,512,128]{3,2,1,0:T(8,128)(2,1)S(1)}, u32[]{:S(2)}, u32[]{:S(2)}) collective-permute-start(bf16[2,2,512,128]{3,2,1,0:T(8,128)(2,1)S(1)} %collective-permute-done.9.refs_1_), channel_id=1, source_target_pairs={{0,2},{2,4},{4,6},{6,8},{8,10},{10,12},{12,14},{14,16},{16,18},{18... | collective-permute-start | bytes 1572872 | tf_op jit(solution)/shard_map/onward_3/ppermute | solution.py:312
  69.5 10.0 %collective-permute-start.8 = (bf16[2,2,384,128]{3,2,1,0:T(8,128)(2,1)S(1)}, bf16[2,2,384,128]{3,2,1,0:T(8,128)(2,1)S(1)}, u32[]{:S(2)}, u32[]{:S(2)}) collective-permute-start(bf16[2,2,384,128]{3,2,1,0:T(8,128)(2,1)S(1)} %collective-permute-done.refs_1_), channel_id=1, source_target_pairs={{0,2},{2,4},{4,6},{6,8},{8,10},{10,12},{12,14},{14,16},{16,18},{18... | collective-permute-start | bytes 1179656 | tf_op jit(solution)/shard_map/onward_4/ppermute | solution.py:312
  71.6 5.8 %collective-permute-start.1 = (bf16[2,2,128,128]{3,2,1,0:T(8,128)(2,1)S(1)}, bf16[2,2,128,128]{3,2,1,0:T(8,128)(2,1)S(1)}, u32[]{:S(2)}, u32[]{:S(2)}) collective-permute-start(bf16[2,2,128,128]{3,2,1,0:T(8,128)(2,1)S(1)} %get-tuple-element.25), channel_id=1, source_target_pairs={{0,1},{1,0},{2,3},{3,2},{4,5},{5,4},{6,7},{7,6},{8,9},{9,8},{10,11... | collective-permute-start | bytes 393224 | tf_op jit(solution)/shard_map/rest_4/ppermute | solution.py:295

commit v3 on v2

--- a/solution.py
+++ b/solution.py
@@ -21,7 +21,7 @@
 
 def split_heads(heads):
     sizes = []
-    for share in (3 / 12, 3 / 12, 2 / 12, 2 / 12):
+    for share in (4 / 12, 3 / 12, 2 / 12, 2 / 12):
         size = min(max(1, round(share * heads)), heads - sum(sizes) - 1)
         if size > 0:
             sizes.append(size)
@@ -90,15 +90,13 @@
         load_v.wait()
         store.start()
     cut_jobs = []
-    if cuts:
-        size = groups[-1][1]
-        spots = cut_spots(rows // TILE, cuts[0])
+    spots = cut_spots(rows // TILE, cuts[0][-1]) if cuts else []
+    for (start, size, which, extent), out in zip(cuts, cut_outs):
+        part = pl.ds(pl.multiple_of(spots[which] * TILE, TILE), extent * TILE)
         for h in range(size):
-            for i, (extent, out) in enumerate(zip(cuts, cut_outs)):
-                part = pl.ds(pl.multiple_of(spots[i] * TILE, TILE), extent * TILE)
-                source = out_buf.at[len(jobs) - size + h, :, part]
-                cut_jobs.append(pltpu.make_async_copy(source, out.at[h], cut_sems.at[h, i]))
-                cut_jobs[-1].start()
+            source = out_buf.at[start - groups[0][0] + h, :, part]
+            cut_jobs.append(pltpu.make_async_copy(source, out.at[h], cut_sems.at[len(cut_jobs)]))
+            cut_jobs[-1].start()
     for load, store in q_jobs:
         load.wait()
         store.start()
@@ -114,9 +112,8 @@
     rows = keys.shape[0]
     heads = sum(size for _, size in groups)
     q_heads = sum(size for _, size in q_groups)
-    last = groups[-1][1]
     shapes = [(size, 2, rows, HD) for _, size in groups] + [(size, rows, HD) for _, size in q_groups]
-    shapes += [(last, 2, extent * TILE, HD) for extent in cuts]
+    shapes += [(size, 2, extent * TILE, HD) for _, size, _, extent in cuts]
     return pl.pallas_call(
         functools.partial(pack_kernel, groups, q_groups, cuts),
         out_shape=[jax.ShapeDtypeStruct(shape, keys.dtype) for shape in shapes],
@@ -128,7 +125,7 @@
             pltpu.VMEM((max(q_heads, 1), rows, HD), keys.dtype),
             pltpu.SemaphoreType.DMA((heads, 3)),
             pltpu.SemaphoreType.DMA((max(q_heads, 1), 2)),
-            pltpu.SemaphoreType.DMA((last, max(len(cuts), 1))),
+            pltpu.SemaphoreType.DMA((max(sum(size for _, size, _, _ in cuts), 1),)),
         ],
         compiler_params=pltpu.CompilerParams(vmem_limit_bytes=limit),
         cost_estimate=pl.CostEstimate(flops=0, bytes_accessed=8 * rows * heads * HD, transcendentals=0),
@@ -136,9 +133,9 @@
 
 
 def attend_kernel(cfg, tiles_ref, counts_ref, q_ref, *refs):
-    low, size, pieces, (hops, rim, relay, parted), early, has_acc, final = cfg
+    low, size, shifts, (hops, rim, relay, parted), early, has_acc, final = cfg
     refs = list(refs)
-    piece_refs = [refs.pop(0) for _ in range(pieces)]
+    piece_refs = [refs.pop(0) for _ in shifts]
     early_refs = [refs.pop(0) for _ in early or ()]
     w_ref = None if early is None else refs.pop(0)
     acc_ref = refs.pop(0) if has_acc else None
@@ -191,7 +188,7 @@
         for i, ref in enumerate(piece_refs):
             place = pl.ds(pl.multiple_of(spots[i] * TILE, TILE), ref.shape[2])
             for part in range(2):
-                kv_buf[h % 2, part, place] = ref[h, part]
+                kv_buf[h % 2, part, place] = ref[h + shifts[i], part]
         kv_buf[h % 2, 1, spans : spans + TILE] = zeros
 
     jobs = [(h, tile) for h in range(size) for tile in range(tiles)]
@@ -224,7 +221,7 @@
         copy.wait()
 
 
-def attend(tile_list, counts, layout, queries, pieces, span, early, out_weight, acc, final):
+def attend(tile_list, counts, layout, queries, pieces, shifts, span, early, out_weight, acc, final):
     rows = queries.shape[1]
     low, size = span
     reach = (2 * layout[0] + 1) * rows
@@ -245,7 +242,7 @@
             scratch += [pltpu.VMEM((rows, width), bf16), pltpu.SemaphoreType.DMA((-(-width // STRIP),))]
     return pl.pallas_call(
         functools.partial(
-            attend_kernel, (low, size, len(pieces), layout, parts, acc is not None, final)
+            attend_kernel, (low, size, shifts, layout, parts, acc is not None, final)
         ),
         out_shape=out_shape,
         in_specs=[SMEM] * 2 + [VMEM] * (len(operands) - 2),
@@ -269,7 +266,6 @@
     hops = -(-REACH // tiles)
     relay = members == 2 and hops == 1
     rim = min(REACH, tiles)
-    cuts = [rim, tiles - rim] if relay and tiles > rim else []
 
     spans, low = [], 0
     for size in split_heads(model // HD):
@@ -277,39 +273,44 @@
         low += size
     count = len(spans)
     sent = pack(queries, keys, values, spans[:1], [], [], VMEM_WHOLE)
+    split = max(1, count - 2) if relay and tiles > rim else count
+    cuts = [(low, size, 0, rim) for low, size in spans[split:]]
+    if cuts:
+        rest_low = spans[split][0]
+        cuts.append((rest_low, model // HD - rest_low, 1, tiles - rim))
     laid = pack(queries, after(keys, *sent), values, spans, spans, cuts, VMEM_LIMIT)
     blocks, heads_of, parts = laid[:count], laid[count : 2 * count], laid[2 * count :]
-    sent = [[block] for block in (*sent, *blocks[1:])]
-    if parts and count > 1:
-        sent[-1] = parts
+    sent = [*sent, *blocks[1:split], *parts]
 
     onward = [(2 * g, 2 * g + 2) for g in range(groups - 1)]
     onward += [(2 * g + 3, 2 * g + 1) for g in range(groups - 1)]
     near = []
-    for i, group_sent in enumerate(sent):
+    for i, block in enumerate(sent):
         if relay:
-            swap = [(0, 1), (1, 0)]
-            near.append([])
-            for name, block in zip(("partner", "rest"), group_sent):
-                with jax.named_scope(f"{name}_{i}"):
-                    near[-1].append(lax.ppermute(block, "ulysses", swap))
+            with jax.named_scope(f"partner_{i}" if i < count else f"rest_{i}"):
+                near.append([lax.ppermute(block, "ulysses", [(0, 1), (1, 0)])])
         else:
             near.append(
                 [
-                    lax.ppermute(group_sent[0], both, [(j, j - o) for j in range(total) if 0 <= j - o < total])
+                    lax.ppermute(block, both, [(j, j - o) for j in range(total) if 0 <= j - o < total])
                     for o in range(-hops, hops + 1)
                     if o
                 ]
             )
 
-    results, acc, mid = [], None, count - 3
+    results, acc, mid = [], None, count - 4
     for i in range(count + 1):
         if i < count:
             pieces = [blocks[i], *near[i]]
+            shifts = [0] * len(pieces)
+            if i >= split:
+                pieces += near[count]
+                shifts.append(spans[i][0] - rest_low)
             if relay:
                 gate = near[i][0] if i < 2 else after(near[i][0], results[i - 2])
                 with jax.named_scope(f"onward_{i}"):
                     pieces.append(lax.ppermute(gate, both, onward))
+                shifts.append(0)
         if i >= 1:
             j = i - 1
             final = i == count
@@ -318,13 +319,13 @@
                 early = results[max(mid + 1, 0) :]
             elif j == mid:
                 early = results[:]
-            layout = (hops, rim, relay, len(sent[j]) > 1)
+            layout = (hops, rim, relay, j >= split)
             with jax.named_scope(f"attend_{j}"):
-                result = attend(tile_list, counts, layout, heads_of[j], held, spans[j], early, out_weight, acc if final else None, final)
+                result = attend(tile_list, counts, layout, heads_of[j], *held, spans[j], early, out_weight, acc if final else None, final)
             results.append(result)
             if j == mid:
                 acc = result
-        held = pieces
+        held = pieces, tuple(shifts)
     return results[-1]
 
 

time: 83.6 us -> 83.2 us (level)
  waiting for transfers between devices: 38.6 us -> 36.7 us
    ppermute x6, waiting for transfers between devices: 36.1 us -> 34.3 us  [on_device(): near.append([lax.ppermute(block, 'ulysses', [(0, 1), (1, 0)])])]
  transfers between devices with their start and end apart: 11 -> 11, of which waited for: 8 -> 7; matrix products, arithmetic and copies ran while one was open for 0% -> 0% of each run, Pallas kernels for 19% -> 20%
where the time goes in v3:
time: 83.2 us; the launch traced here: 82.9 us
  waiting for transfers between devices  36.7 us (44%)
  Pallas kernels  22.4 us (27%)
  starting transfers between devices  19.2 us (23%)
  local copies, waits for them, and re-layouts  4.24 us (5%)
    ppermute x6, waiting for transfers between devices, on_device(): near.append([lax.ppermute(block, 'ulysses', [(0, 1), (1, 0)])])  34.3 us
    pallas_call x5, Pallas kernels, attend(): pl.pallas_call(functools.partial(attend_kernel, (low, size, shifts, layou...  14.8 us
    ppermute x5, starting transfers between devices, on_device(): pieces.append(lax.ppermute(gate, both, onward))  9.74 us
    ppermute x6, starting transfers between devices, on_device(): near.append([lax.ppermute(block, 'ulysses', [(0, 1), (1, 0)])])  9.51 us
    pallas_call x2, Pallas kernels, pack(): pl.pallas_call(functools.partial(pack_kernel, groups, q_groups, cuts), ou...  7.57 us
    unnamed x14, local copies, waits for them, and re-layouts  4.24 us
    ppermute x5, waiting for transfers between devices, on_device(): pieces.append(lax.ppermute(gate, both, onward))  2.44 us
  transfers between devices with their start and end apart: 11, of which 7 were waited for; matrix products, arithmetic and copies ran while one was open for 0% of the time, Pallas kernels for 20%

profile of v3, /device:TPU:8, one launch (start us, length us, event | category | flops | bytes accessed | tf_op | source)
XLA Modules:
  0.0 82.9 jit_solution(11422384408581478416)
XLA Ops:
  0.0 2.2 %shard_map.64 = bf16[4,2,512,128]{3,2,1,0:T(8,128)(2,1)} custom-call(bf16[512,1536]{1,0:T(8,128)(2,1)} %refs_0_.3, bf16[512,1536]{1,0:T(8,128)(2,1)} %refs_1_.2, bf16[512,1536]{1,0:T(8,128)(2,1)} %refs_2_.3), custom_call_target="tpu_custom_call" | custom-call | bytes 2097152 | tf_op jit(solution)/shard_map/pallas_call | solution.py:117
  2.3 1.6 %collective-permute-start.3 = (bf16[4,2,512,128]{3,2,1,0:T(8,128)(2,1)}, bf16[4,2,512,128]{3,2,1,0:T(8,128)(2,1)S(1)}, u32[]{:S(2)}, u32[]{:S(2)}) collective-permute-start(bf16[4,2,512,128]{3,2,1,0:T(8,128)(2,1)} %shard_map.64), channel_id=1, source_target_pairs={{0,1},{1,0},{2,3},{3,2},{4,5},{5,4},{6,7},{7,6},{8,9},{9,8},{10,11... | collective-permute-start | bytes 3145736 | tf_op jit(solution)/shard_map/partner_0/ppermute | solution.py:291
  3.8 1.4 %copy-done = bf16[512,1536]{1,0:T(8,128)(2,1)S(1)} copy-done((bf16[512,1536]{1,0:T(8,128)(2,1)S(1)}, bf16[512,1536]{1,0:T(8,128)(2,1)}, u32[]{:S(2)}) %copy-start) | copy-done | bytes 1572888
  5.2 1.4 %copy-done.1 = bf16[512,1536]{1,0:T(8,128)(2,1)S(1)} copy-done((bf16[512,1536]{1,0:T(8,128)(2,1)S(1)}, bf16[512,1536]{1,0:T(8,128)(2,1)}, u32[]{:S(2)}) %copy-start.1) | copy-done | bytes 1572888
  6.6 1.4 %copy-done.2 = bf16[512,1536]{1,0:T(8,128)(2,1)S(1)} copy-done((bf16[512,1536]{1,0:T(8,128)(2,1)S(1)}, bf16[512,1536]{1,0:T(8,128)(2,1)}, u32[]{:S(2)}) %copy-start.2) | copy-done | bytes 1572888
  8.1 5.3 %shard_map.65 = (bf16[4,2,512,128]{3,2,1,0:T(8,128)(2,1)S(1)}, bf16[3,2,512,128]{3,2,1,0:T(8,128)(2,1)S(1)}, bf16[2,2,512,128]{3,2,1,0:T(8,128)(2,1)S(1)}, bf16[...) custom-call(bf16[512,1536]{1,0:T(8,128)(2,1)S(1)} %copy-done, ...), custom_call_target="tpu_custom_call" | custom-call | bytes 6291456 | tf_op jit(solution)/shard_map/pallas_call | solution.py:117
  14.3 14.3 %collective-permute-done.3.refs_1_ = bf16[4,2,512,128]{3,2,1,0:T(8,128)(2,1)S(1)} collective-permute-done((bf16[4,2,512,128]{3,2,1,0:T(8,128)(2,1)}, bf16[4,2,512,128]{3,2,1,0:T(8,128)(2,1)S(1)}, u32[]{:S(2)}, u32[]{:S(2)}) %collective-permute-start.3) | collective-permute-done | bytes 1048608 | tf_op jit(solution)/shard_map/partner_0/ppermute | solution.py:291
  28.6 1.9 %collective-permute-start.4 = (bf16[4,2,512,128]{3,2,1,0:T(8,128)(2,1)S(1)}, bf16[4,2,512,128]{3,2,1,0:T(8,128)(2,1)S(1)}, u32[]{:S(2)}, u32[]{:S(2)}) collective-permute-start(bf16[4,2,512,128]{3,2,1,0:T(8,128)(2,1)S(1)} %collective-permute-done.3.refs_1_), channel_id=1, source_target_pairs={{0,2},{2,4},{4,6},{6,8},{8,10},{10,12},{12,14},{14,16},{16,18},{18... | collective-permute-start | bytes 3145736 | tf_op jit(solution)/shard_map/onward_0/ppermute | solution.py:312
  30.5 1.6 %collective-permute-start.2 = (bf16[2,2,512,128]{3,2,1,0:T(8,128)(2,1)S(1)}, bf16[2,2,512,128]{3,2,1,0:T(8,128)(2,1)S(1)}, u32[]{:S(2)}, u32[]{:S(2)}) collective-permute-start(bf16[2,2,512,128]{3,2,1,0:T(8,128)(2,1)S(1)} %get-tuple-element.28.refs_0_), channel_id=1, source_target_pairs={{0,1},{1,0},{2,3},{3,2},{4,5},{5,4},{6,7},{7,6},{8,9},{9,8},{10,11... | collective-permute-start | bytes 1572872 | tf_op jit(solution)/shard_map/partner_2/ppermute | solution.py:291
  32.1 13.4 %collective-permute-done.8.refs_1_ = bf16[3,2,512,128]{3,2,1,0:T(8,128)(2,1)S(1)} collective-permute-done((bf16[3,2,512,128]{3,2,1,0:T(8,128)(2,1)S(1)}, bf16[3,2,512,128]{3,2,1,0:T(8,128)(2,1)S(1)}, u32[]{:S(2)}, u32[]{:S(2)}) %collective-permute-start.8) | collective-permute-done | bytes 786464 | tf_op jit(solution)/shard_map/partner_1/ppermute | solution.py:291
  45.4 1.9 %collective-permute-start.9 = (bf16[3,2,512,128]{3,2,1,0:T(8,128)(2,1)S(1)}, bf16[3,2,512,128]{3,2,1,0:T(8,128)(2,1)S(1)}, u32[]{:S(2)}, u32[]{:S(2)}) collective-permute-start(bf16[3,2,512,128]{3,2,1,0:T(8,128)(2,1)S(1)} %collective-permute-done.8.refs_1_), channel_id=1, source_target_pairs={{0,2},{2,4},{4,6},{6,8},{8,10},{10,12},{12,14},{14,16},{16,18},{18... | collective-permute-start | bytes 2359304 | tf_op jit(solution)/shard_map/onward_1/ppermute | solution.py:312
  47.4 1.6 %collective-permute-start.7 = (bf16[2,2,384,128]{3,2,1,0:T(8,128)(2,1)S(1)}, bf16[2,2,384,128]{3,2,1,0:T(8,128)(2,1)S(1)}, u32[]{:S(2)}, u32[]{:S(2)}) collective-permute-start(bf16[2,2,384,128]{3,2,1,0:T(8,128)(2,1)S(1)} %get-tuple-element.35), channel_id=1, source_target_pairs={{0,1},{1,0},{2,3},{3,2},{4,5},{5,4},{6,7},{7,6},{8,9},{9,8},{10,11... | collective-permute-start | bytes 1179656 | tf_op jit(solution)/shard_map/partner_3/ppermute | solution.py:291
  48.9 3.1 %attend_0.1.refs_3_ = bf16[512,512]{1,0:T(8,128)(2,1)S(1)} custom-call(s32[8,5]{1,0:T(8,128)S(1)} %copy-done.3, s32[8]{0:T(128)S(1)} %copy-done.4, bf16[4,512,128]{2,1,0:T(8,128)(2,1)S(1)} %get-tuple-element.29.q_ref, bf16[4,2,512,128]{3,2,1,0:T(8,128)(2,1)S(1)} %get-tuple-element.30.refs_0_, bf16[4,2,512,128]{3,2,1,0:T(8,128)(2,1)S(1)} %collective-permute-done.3.refs_1_, ...), custom_call_target="tpu_custom_call" | custom-call | tf_op jit(solution)/shard_map/attend_0/pallas_call | solution.py:243
  52.0 4.6 %collective-permute-done.2.refs_1_ = bf16[2,2,512,128]{3,2,1,0:T(8,128)(2,1)S(1)} collective-permute-done((bf16[2,2,512,128]{3,2,1,0:T(8,128)(2,1)S(1)}, bf16[2,2,512,128]{3,2,1,0:T(8,128)(2,1)S(1)}, u32[]{:S(2)}, u32[]{:S(2)}) %collective-permute-start.2) | collective-permute-done | bytes 524320 | tf_op jit(solution)/shard_map/partner_2/ppermute | solution.py:291
  56.7 1.9 %collective-permute-start.5 = (bf16[2,2,512,128]{3,2,1,0:T(8,128)(2,1)S(1)}, bf16[2,2,512,128]{3,2,1,0:T(8,128)(2,1)S(1)}, u32[]{:S(2)}, u32[]{:S(2)}) collective-permute-start(bf16[2,2,512,128]{3,2,1,0:T(8,128)(2,1)S(1)} %collective-permute-done.2.refs_1_), channel_id=1, source_target_pairs={{0,2},{2,4},{4,6},{6,8},{8,10},{10,12},{12,14},{14,16},{16,18},{18... | collective-permute-start | bytes 1572872 | tf_op jit(solution)/shard_map/onward_2/ppermute | solution.py:312
  58.6 1.6 %collective-permute-start = (bf16[1,2,384,128]{3,2,1,0:T(8,128)(2,1)S(1)}, bf16[1,2,384,128]{3,2,1,0:T(8,128)(2,1)S(1)}, u32[]{:S(2)}, u32[]{:S(2)}) collective-permute-start(bf16[1,2,384,128]{3,2,1,0:T(8,128)(2,1)S(1)} %get-tuple-element.25), channel_id=1, source_target_pairs={{0,1},{1,0},{2,3},{3,2},{4,5},{5,4},{6,7},{7,6},{8,9},{9,8},{10,11... | collective-permute-start | bytes 589832 | tf_op jit(solution)/shard_map/partner_4/ppermute | solution.py:291
  60.2 4.2 %attend_1.1.refs_7_ = f32[512,1536]{1,0:T(8,128)S(1)} custom-call(s32[8,5]{1,0:T(8,128)S(1)} %copy-done.3, s32[8]{0:T(128)S(1)} %copy-done.4, bf16[3,512,128]{2,1,0:T(8,128)(2,1)S(1)} %get-tuple-element.36.q_ref, bf16[3,2,512,128]{3,2,1,0:T(8,128)(2,1)S(1)} %get-tuple-element.37.refs_0_, bf16[3,2,512,128]{3,2,1,0:T(8,128)(2,1)S(1)} %collective-permute-done.8.refs_1_, ...), custom_call_target="tpu_custom_call" | custom-call | tf_op jit(solution)/shard_map/attend_1/pallas_call | solution.py:243
  65.0 1.9 %collective-permute-start.10 = (bf16[2,2,384,128]{3,2,1,0:T(8,128)(2,1)S(1)}, bf16[2,2,384,128]{3,2,1,0:T(8,128)(2,1)S(1)}, u32[]{:S(2)}, u32[]{:S(2)}) collective-permute-start(bf16[2,2,384,128]{3,2,1,0:T(8,128)(2,1)S(1)} %collective-permute-done.7.refs_1_), channel_id=1, source_target_pairs={{0,2},{2,4},{4,6},{6,8},{8,10},{10,12},{12,14},{14,16},{16,18},{18... | collective-permute-start | bytes 1179656 | tf_op jit(solution)/shard_map/onward_3/ppermute | solution.py:312
  66.9 2.4 %collective-permute-start.1 = (bf16[3,2,128,128]{3,2,1,0:T(8,128)(2,1)S(1)}, bf16[3,2,128,128]{3,2,1,0:T(8,128)(2,1)S(1)}, u32[]{:S(2)}, u32[]{:S(2)}) collective-permute-start(bf16[3,2,128,128]{3,2,1,0:T(8,128)(2,1)S(1)} %get-tuple-element.26), channel_id=1, source_target_pairs={{0,1},{1,0},{2,3},{3,2},{4,5},{5,4},{6,7},{7,6},{8,9},{9,8},{10,11... | collective-permute-start | bytes 589832 | tf_op jit(solution)/shard_map/rest_5/ppermute | solution.py:291
  69.3 2.0 %attend_2.1.refs_4_ = bf16[512,256]{1,0:T(8,128)(2,1)S(1)} custom-call(s32[8,5]{1,0:T(8,128)S(1)} %copy-done.3, s32[8]{0:T(128)S(1)} %copy-done.4, bf16[2,512,128]{2,1,0:T(8,128)(2,1)S(1)} %get-tuple-element.27.q_ref, bf16[2,2,512,128]{3,2,1,0:T(8,128)(2,1)S(1)} %get-tuple-element.28.refs_0_, bf16[2,2,512,128]{3,2,1,0:T(8,128)(2,1)S(1)} %collective-permute-done.2.refs_1_, ...), custom_call_target="tpu_custom_call" | custom-call | tf_op jit(solution)/shard_map/attend_2/pallas_call | solution.py:243
  71.3 2.1 %collective-permute-start.6 = (bf16[1,2,384,128]{3,2,1,0:T(8,128)(2,1)S(1)}, bf16[1,2,384,128]{3,2,1,0:T(8,128)(2,1)S(1)}, u32[]{:S(2)}, u32[]{:S(2)}) collective-permute-start(bf16[1,2,384,128]{3,2,1,0:T(8,128)(2,1)S(1)} %collective-permute-done.refs_1_), channel_id=1, source_target_pairs={{0,2},{2,4},{4,6},{6,8},{8,10},{10,12},{12,14},{14,16},{16,18},{18... | collective-permute-start | bytes 589832 | tf_op jit(solution)/shard_map/onward_4/ppermute | solution.py:312
  75.0 2.0 %attend_3.1.refs_5_ = bf16[512,256]{1,0:T(8,128)(2,1)S(1)} custom-call(s32[8,5]{1,0:T(8,128)S(1)} %copy-done.3, s32[8]{0:T(128)S(1)} %copy-done.4, bf16[2,512,128]{2,1,0:T(8,128)(2,1)S(1)} %get-tuple-element.33.q_ref, bf16[2,2,512,128]{3,2,1,0:T(8,128)(2,1)S(1)} %get-tuple-element.34.refs_0_, bf16[2,2,384,128]{3,2,1,0:T(8,128)(2,1)S(1)} %collective-permute-done.7.refs_1_, ...), custom_call_target="tpu_custom_call" | custom-call | tf_op jit(solution)/shard_map/attend_3/pallas_call | solution.py:243
  77.0 2.2 %collective-permute-done.6.refs_3_ = bf16[1,2,384,128]{3,2,1,0:T(8,128)(2,1)S(1)} collective-permute-done((bf16[1,2,384,128]{3,2,1,0:T(8,128)(2,1)S(1)}, bf16[1,2,384,128]{3,2,1,0:T(8,128)(2,1)S(1)}, u32[]{:S(2)}, u32[]{:S(2)}) %collective-permute-start.6) | collective-permute-done | bytes 196640 | tf_op jit(solution)/shard_map/onward_4/ppermute | solution.py:312
  79.2 3.5 %attend_4.1 = bf16[512,1536]{1,0:T(8,128)(2,1)} custom-call(s32[8,5]{1,0:T(8,128)S(1)} %copy-done.3, s32[8]{0:T(128)S(1)} %copy-done.4, bf16[1,512,128]{2,1,0:T(8,128)(2,1)S(1)} %get-tuple-element.23.q_ref, bf16[1,2,512,128]{3,2,1,0:T(8,128)(2,1)S(1)} %get-tuple-element.24.refs_0_, bf16[1,2,384,128]{3,2,1,0:T(8,128)(2,1)S(1)} %collective-permute-done.refs_1_, ...), custom_call_target="tpu_custom_call" | custom-call | tf_op jit(solution)/shard_map/attend_4/pallas_call | solution.py:243
  (20 shorter events, 3.1 us)
Async XLA Ops:
  0.0 60.2 %slice-start = ((s8[4718592]{0:T(1024)(128)(4,1)}), s8[524288]{0:T(1024)(128)(4,1)S(1)}, s32[]{:S(2)}) async-start(s8[4718592]{0:T(1024)(128)(4,1)} %bitcast), calls=%async_computation | async-start | bytes 1048576
  2.3 57.9 %slice-start.1 = ((s8[4718592]{0:T(1024)(128)(4,1)}), s8[4194304]{0:T(1024)(128)(4,1)S(1)}, s32[]{:S(2)}) async-start(s8[4718592]{0:T(1024)(128)(4,1)} %bitcast), calls=%async_computation.1 | async-start | bytes 8388608
  2.3 26.3 %collective-permute-start.3 = (bf16[4,2,512,128]{3,2,1,0:T(8,128)(2,1)}, bf16[4,2,512,128]{3,2,1,0:T(8,128)(2,1)S(1)}, u32[]{:S(2)}, u32[]{:S(2)}) collective-permute-start(bf16[4,2,512,128]{3,2,1,0:T(8,128)(2,1)} %shard_map.64), channel_id=1, source_target_pairs={{0,1},{1,0},{2,3},{3,2},{4,5},{5,4},{6,7},{7,6},{8,9},{9,8},{10,11... | collective-permute-start | bytes 3145736 | tf_op jit(solution)/shard_map/partner_0/ppermute | solution.py:291
  3.8 1.4 %copy-start = (bf16[512,1536]{1,0:T(8,128)(2,1)S(1)}, bf16[512,1536]{1,0:T(8,128)(2,1)}, u32[]{:S(2)}) copy-start(bf16[512,1536]{1,0:T(8,128)(2,1)} %refs_0_.3) | copy-start | bytes 4718596
  5.2 1.4 %copy-start.1 = (bf16[512,1536]{1,0:T(8,128)(2,1)S(1)}, bf16[512,1536]{1,0:T(8,128)(2,1)}, u32[]{:S(2)}) copy-start(bf16[512,1536]{1,0:T(8,128)(2,1)} %refs_1_.2) | copy-start | bytes 4718596
  6.6 1.4 %copy-start.2 = (bf16[512,1536]{1,0:T(8,128)(2,1)S(1)}, bf16[512,1536]{1,0:T(8,128)(2,1)}, u32[]{:S(2)}) copy-start(bf16[512,1536]{1,0:T(8,128)(2,1)} %refs_2_.3) | copy-start | bytes 4718596
  8.0 40.9 %copy-start.3 = (s32[8,5]{1,0:T(8,128)S(1)}, s32[8,5]{1,0:T(8,128)}, u32[]{:S(2)}) copy-start(s32[8,5]{1,0:T(8,128)} %tiles_ref.9) | copy-start | bytes 484
  8.1 40.9 %copy-start.4 = (s32[8]{0:T(128)S(1)}, s32[8]{0:T(128)}, u32[]{:S(2)}) copy-start(s32[8]{0:T(128)} %counts_ref.9) | copy-start | bytes 100
  13.4 32.1 %collective-permute-start.8 = (bf16[3,2,512,128]{3,2,1,0:T(8,128)(2,1)S(1)}, bf16[3,2,512,128]{3,2,1,0:T(8,128)(2,1)S(1)}, u32[]{:S(2)}, u32[]{:S(2)}) collective-permute-start(bf16[3,2,512,128]{3,2,1,0:T(8,128)(2,1)S(1)} %get-tuple-element.37.refs_0_), channel_id=1, source_target_pairs={{0,1},{1,0},{2,3},{3,2},{4,5},{5,4},{6,7},{7,6},{8,9},{9,8},{10,11... | collective-permute-start | bytes 2359304 | tf_op jit(solution)/shard_map/partner_1/ppermute | solution.py:291
  28.6 20.3 %collective-permute-start.4 = (bf16[4,2,512,128]{3,2,1,0:T(8,128)(2,1)S(1)}, bf16[4,2,512,128]{3,2,1,0:T(8,128)(2,1)S(1)}, u32[]{:S(2)}, u32[]{:S(2)}) collective-permute-start(bf16[4,2,512,128]{3,2,1,0:T(8,128)(2,1)S(1)} %collective-permute-done.3.refs_1_), channel_id=1, source_target_pairs={{0,2},{2,4},{4,6},{6,8},{8,10},{10,12},{12,14},{14,16},{16,18},{18... | collective-permute-start | bytes 3145736 | tf_op jit(solution)/shard_map/onward_0/ppermute | solution.py:312
  30.5 26.2 %collective-permute-start.2 = (bf16[2,2,512,128]{3,2,1,0:T(8,128)(2,1)S(1)}, bf16[2,2,512,128]{3,2,1,0:T(8,128)(2,1)S(1)}, u32[]{:S(2)}, u32[]{:S(2)}) collective-permute-start(bf16[2,2,512,128]{3,2,1,0:T(8,128)(2,1)S(1)} %get-tuple-element.28.refs_0_), channel_id=1, source_target_pairs={{0,1},{1,0},{2,3},{3,2},{4,5},{5,4},{6,7},{7,6},{8,9},{9,8},{10,11... | collective-permute-start | bytes 1572872 | tf_op jit(solution)/shard_map/partner_2/ppermute | solution.py:291
  45.4 14.7 %collective-permute-start.9 = (bf16[3,2,512,128]{3,2,1,0:T(8,128)(2,1)S(1)}, bf16[3,2,512,128]{3,2,1,0:T(8,128)(2,1)S(1)}, u32[]{:S(2)}, u32[]{:S(2)}) collective-permute-start(bf16[3,2,512,128]{3,2,1,0:T(8,128)(2,1)S(1)} %collective-permute-done.8.refs_1_), channel_id=1, source_target_pairs={{0,2},{2,4},{4,6},{6,8},{8,10},{10,12},{12,14},{14,16},{16,18},{18... | collective-permute-start | bytes 2359304 | tf_op jit(solution)/shard_map/onward_1/ppermute | solution.py:312
  47.4 17.6 %collective-permute-start.7 = (bf16[2,2,384,128]{3,2,1,0:T(8,128)(2,1)S(1)}, bf16[2,2,384,128]{3,2,1,0:T(8,128)(2,1)S(1)}, u32[]{:S(2)}, u32[]{:S(2)}) collective-permute-start(bf16[2,2,384,128]{3,2,1,0:T(8,128)(2,1)S(1)} %get-tuple-element.35), channel_id=1, source_target_pairs={{0,1},{1,0},{2,3},{3,2},{4,5},{5,4},{6,7},{7,6},{8,9},{9,8},{10,11... | collective-permute-start | bytes 1179656 | tf_op jit(solution)/shard_map/partner_3/ppermute | solution.py:291
  56.7 12.6 %collective-permute-start.5 = (bf16[2,2,512,128]{3,2,1,0:T(8,128)(2,1)S(1)}, bf16[2,2,512,128]{3,2,1,0:T(8,128)(2,1)S(1)}, u32[]{:S(2)}, u32[]{:S(2)}) collective-permute-start(bf16[2,2,512,128]{3,2,1,0:T(8,128)(2,1)S(1)} %collective-permute-done.2.refs_1_), channel_id=1, source_target_pairs={{0,2},{2,4},{4,6},{6,8},{8,10},{10,12},{12,14},{14,16},{16,18},{18... | collective-permute-start | bytes 1572872 | tf_op jit(solution)/shard_map/onward_2/ppermute | solution.py:312
  58.6 12.7 %collective-permute-start = (bf16[1,2,384,128]{3,2,1,0:T(8,128)(2,1)S(1)}, bf16[1,2,384,128]{3,2,1,0:T(8,128)(2,1)S(1)}, u32[]{:S(2)}, u32[]{:S(2)}) collective-permute-start(bf16[1,2,384,128]{3,2,1,0:T(8,128)(2,1)S(1)} %get-tuple-element.25), channel_id=1, source_target_pairs={{0,1},{1,0},{2,3},{3,2},{4,5},{5,4},{6,7},{7,6},{8,9},{9,8},{10,11... | collective-permute-start | bytes 589832 | tf_op jit(solution)/shard_map/partner_4/ppermute | solution.py:291
  65.0 10.0 %collective-permute-start.10 = (bf16[2,2,384,128]{3,2,1,0:T(8,128)(2,1)S(1)}, bf16[2,2,384,128]{3,2,1,0:T(8,128)(2,1)S(1)}, u32[]{:S(2)}, u32[]{:S(2)}) collective-permute-start(bf16[2,2,384,128]{3,2,1,0:T(8,128)(2,1)S(1)} %collective-permute-done.7.refs_1_), channel_id=1, source_target_pairs={{0,2},{2,4},{4,6},{6,8},{8,10},{10,12},{12,14},{14,16},{16,18},{18... | collective-permute-start | bytes 1179656 | tf_op jit(solution)/shard_map/onward_3/ppermute | solution.py:312
  66.9 7.9 %collective-permute-start.1 = (bf16[3,2,128,128]{3,2,1,0:T(8,128)(2,1)S(1)}, bf16[3,2,128,128]{3,2,1,0:T(8,128)(2,1)S(1)}, u32[]{:S(2)}, u32[]{:S(2)}) collective-permute-start(bf16[3,2,128,128]{3,2,1,0:T(8,128)(2,1)S(1)} %get-tuple-element.26), channel_id=1, source_target_pairs={{0,1},{1,0},{2,3},{3,2},{4,5},{5,4},{6,7},{7,6},{8,9},{9,8},{10,11... | collective-permute-start | bytes 589832 | tf_op jit(solution)/shard_map/rest_5/ppermute | solution.py:291
  71.3 7.9 %collective-permute-start.6 = (bf16[1,2,384,128]{3,2,1,0:T(8,128)(2,1)S(1)}, bf16[1,2,384,128]{3,2,1,0:T(8,128)(2,1)S(1)}, u32[]{:S(2)}, u32[]{:S(2)}) collective-permute-start(bf16[1,2,384,128]{3,2,1,0:T(8,128)(2,1)S(1)} %collective-permute-done.refs_1_), channel_id=1, source_target_pairs={{0,2},{2,4},{4,6},{6,8},{8,10},{10,12},{12,14},{14,16},{16,18},{18... | collective-permute-start | bytes 589832 | tf_op jit(solution)/shard_map/onward_4/ppermute | solution.py:312
